TPU v7x, 32 devices: a whole 2x2x4 slice. The times are simulated.
32 devices in a mesh: tm: 4 (over y, x), sta: 8 (over z, core).
Axes of the slice: x: 2, y: 2, z: 4, core: 2. Of those that a mesh axis runs over, the one named last changes fastest.
Arguments:
- spectra: bfloat16 [4, 8, 2, 3, 2, 2048], P('tm', 'sta'), may hold values from -6 to 6
- pair_blocks: int32 [8, 8, 2], P('sta'), may hold values from 0 to 7, as said below
- block_count: int32 [8], P('sta'), may hold values from 1 to 8, as said below
Outputs:
- correlations: bfloat16 [8, 8, 1, 1, 3, 3, 4096], P('sta', 'tm')
Inputs may be any that keep to these rules, and one draw needn't show every extreme that they name: `pair_blocks`: among the first block_count[o] slots of all owners o, every unordered pair of two different station groups stands exactly once, in either order; later slots hold arbitrary group numbers. `block_count`: the counts sum to 28, and one owner uses all 8 slots.
All inputs are finite; a program needn't handle non-finite values.
Results may differ from a plain program's by a relative error of at most 0.014.
Values may be sent and summed in bfloat16 or wider, within the bound.
No kernel may reach another device: no remote copies, remote signals or barrier semaphores. Data moves between devices by JAX's collectives and lax.ppermute only.
A program may use at most 64 MiB of HBM per device.

v0:
```python
import math

import jax
import jax.numpy as jnp
from jax import lax
from jax.sharding import PartitionSpec as P

SMOOTH = 64


epsilon = 1e-05
radix_count = 64


def whiten(spectra):
    values = spectra.astype(jnp.float32)
    amplitude = jnp.sqrt(values[..., 0, :] ** 2 + values[..., 1, :] ** 2)
    width = amplitude.shape[-1]
    padding = [(0, 0)] * (amplitude.ndim - 1) + [(SMOOTH + 1, SMOOTH)]
    running = jnp.cumsum(jnp.pad(amplitude, padding), axis=-1)
    window_sum = running[..., 2 * SMOOTH + 1 :] - running[..., :width]
    positions = jnp.arange(width, dtype=jnp.int32)
    lower = jnp.maximum(positions - SMOOTH, 0)
    upper = jnp.minimum(positions + SMOOTH, width - 1)
    bin_count = (upper - lower + 1).astype(jnp.float32)
    smoothed = window_sum / bin_count
    white = values / (smoothed + epsilon)[..., None, :]
    return white.astype(jnp.bfloat16)


def cross_hours(every, chosen, group_size):
    grouped = every.reshape(
        every.shape[0],
        every.shape[1] // group_size,
        group_size,
        every.shape[2],
        3,
        2,
        every.shape[-1],
    )
    left = grouped[:, chosen[:, 0]]
    right = grouped[:, chosen[:, 1]]
    real_part = None
    imag_part = None
    for segment in range(grouped.shape[3]):
        left_seg = left[:, :, :, segment].astype(jnp.float32)
        right_seg = right[:, :, :, segment].astype(jnp.float32)
        left_re = left_seg[:, :, :, None, :, None, 0, :]
        left_im = left_seg[:, :, :, None, :, None, 1, :]
        right_re = right_seg[:, :, None, :, None, :, 0, :]
        right_im = right_seg[:, :, None, :, None, :, 1, :]
        real_term = left_re * right_re + left_im * right_im
        imag_term = left_re * right_im - left_im * right_re
        if real_part is None:
            real_part, imag_part = (real_term, imag_term)
        else:
            real_part = real_part + real_term
            imag_part = imag_part + imag_term
    return jnp.stack([real_part, imag_part], axis=-2)


def mask_slots(stack, first_slot, live_count):
    slot_numbers = first_slot + jnp.arange(stack.shape[0], dtype=jnp.int32)
    live = (slot_numbers < live_count).astype(jnp.float32)
    return stack * live[:, None, None, None, None, None, None]


def lag_values(daily):
    width = daily.shape[-1]
    lag_total = 2 * width
    coarse_bins = width // radix_count
    period = lag_total // radix_count
    high = lax.Precision.HIGHEST
    flat_rows = daily.reshape(-1, 2, width).astype(jnp.float32)
    row_total = flat_rows.shape[0]
    real_input = flat_rows[:, 0].reshape(row_total, coarse_bins, radix_count)
    imag_input = flat_rows[:, 1].reshape(row_total, coarse_bins, radix_count)
    coarse_index = jnp.arange(coarse_bins, dtype=jnp.int32)[:, None]
    phase_index = jnp.arange(period, dtype=jnp.int32)[None, :]
    turns_first = coarse_index * phase_index % period
    angle_first = turns_first.astype(jnp.float32) * (2.0 * math.pi / period)
    cos_first = jnp.cos(angle_first)
    sin_first = jnp.sin(angle_first)
    form_first = "rgf,gp->rfp"
    middle_re = jnp.einsum(form_first, real_input, cos_first, precision=high) - jnp.einsum(
        form_first, imag_input, sin_first, precision=high
    )
    middle_im = jnp.einsum(form_first, real_input, sin_first, precision=high) + jnp.einsum(
        form_first, imag_input, cos_first, precision=high
    )
    fine_index = jnp.arange(radix_count, dtype=jnp.int32)[:, None, None]
    block_index = jnp.arange(radix_count, dtype=jnp.int32)[None, :, None]
    inner_index = jnp.arange(period, dtype=jnp.int32)[None, None, :]
    lag_shifted = block_index * period + inner_index - width + lag_total
    turns_second = fine_index * lag_shifted % lag_total
    angle_second = turns_second.astype(jnp.float32) * (2.0 * math.pi / lag_total)
    cos_second = jnp.cos(angle_second)
    sin_second = jnp.sin(angle_second)
    form_second = "rfp,fqp->rqp"
    joined = jnp.einsum(form_second, middle_re, cos_second, precision=high) - jnp.einsum(
        form_second, middle_im, sin_second, precision=high
    )
    scaled = joined.reshape(row_total, lag_total) * width ** (-0.5)
    return scaled.reshape(daily.shape[:-2] + (lag_total,)).astype(jnp.bfloat16)


def body(spectra, pair_blocks, block_count):
    group_size = spectra.shape[1]
    white = whiten(spectra)
    blocks = pair_blocks[0]
    live_count = block_count[0]
    share = blocks.shape[0] // lax.axis_size("tm")
    local_hours = lax.all_gather(white, "tm", axis=0, tiled=True)
    every = lax.all_gather(local_hours, "sta", axis=1, tiled=True)
    first_slot = lax.axis_index("tm") * share
    chosen = lax.dynamic_slice_in_dim(blocks, first_slot, share, 0)
    partial_value = cross_hours(every, chosen, group_size).astype(jnp.bfloat16)
    daily = jnp.sum(partial_value.astype(jnp.float32), axis=0)
    daily = mask_slots(daily, first_slot, live_count)
    return lag_values(daily.astype(jnp.bfloat16))[None]


def solution(mesh):
    placed = (P("tm", "sta", None, None, None, None), P("sta", None, None), P("sta"))
    return jax.shard_map(
        body,
        mesh=mesh,
        in_specs=placed,
        out_specs=P("sta", "tm", None, None, None, None, None),
        check_vma=False,
    )
```

profile of v0, /device:TPU:0, one launch (start us, length us, event | category | flops | bytes accessed | tf_op | source)
XLA Modules:
  0.0 90.5 jit_solution(5996852486791594885)
XLA Ops:
  6.5 0.0 copy-start
  6.5 0.0 copy-start.1
  6.5 0.0 all-gather.2.cloned.1.call-start
  6.6 0.9 convert_element_type.138
  7.4 0.2 sqrt_bitcast_fusion
  7.6 0.2 pad_reduce_fusion
  7.9 1.7 %reduce-window.6 = f32[1,1,2,3,18,128]{5,4,3,2,1,0:T(8,128)S(1)} reduce-window(f32[1,1,2,3,18,128]{5,4,3,2,1,0:T(8,128)S(1)} %reshape.356, f32[]{:T(128)} %constant.59.clone.1), window={size=1x1x1x1x1x128 pad=0_0x0_0x0_0x0_0x0_0x127_0}, to_apply=%region_0.1 | reduce-window | flops 1755648 | bytes 110596 | tf_op jit(solution)/shard_map/reduce-window
  9.6 0.1 slice.97
  9.7 0.1 copy.62
  9.9 0.4 reduce-window.9
  10.2 0.1 broadcast.381
  10.4 0.1 add_bitcast_fusion
  10.6 0.0 copy-done.1
  10.6 0.1 divide_convert_fusion
  10.7 10.9 %all_gather.6 = bf16[4,1,2,3,2,2048]{5,4,3,2,1,0:T(2,128)(2,1)} all-gather(bf16[1,1,2,3,2,2048]{5,4,3,2,1,0:T(2,128)(2,1)S(1)} %divide_convert_fusion), channel_id=1, replica_groups=mesh['tm'=4,'sta'=8] {'tm'}, dimensions={0}, use_global_device_ids=true | all-gather | bytes 245760 | tf_op jit(solution)/shard_map/all_gather | solution.py:113
  21.5 0.0 all-gather.2.cloned.1.call-update
  22.2 0.0 copy-done
  22.2 0.1 constant_dynamic-slice_fusion
  22.3 0.1 copy.66
  22.4 0.1 mul.382
  22.5 0.1 mul.383
  22.6 0.2 fusion.56
  22.8 24.3 %all-gather.2.cloned.1.call-done = bf16[4,8,2,3,2,2048]{5,4,3,2,1,0:T(2,128)(2,1)} async-done(((bf16[4,1,2,3,2,2048]{5,4,3,2,1,0:T(2,128)(2,1)}), bf16[4,8,2,3,2,2048]{5,4,3,2,1,0:T(2,128)(2,1)}) %all-gather.2.cloned.1.call-update) | async-done | bytes 1572880 | tf_op jit(solution)/shard_map/all_gather | solution.py:114
  47.0 2.7 %gather_fusion = bf16[2,4,2,3,2,2048]{5,4,3,2,1,0:T(2,128)(2,1)S(1)} fusion(bf16[4,8,2,3,2,2048]{5,4,3,2,1,0:T(2,128)(2,1)} %all-gather.2.cloned.1.call-done, s32[1024]{0:T(1024)S(1)} %get-tuple-element.24), kind=kCustom, calls=%fused_computation | custom fusion | bytes 786440 | tf_op jit(solution)/shard_map/gather | solution.py:41
  49.8 0.4 fusion.30
  50.2 0.3 fusion.82
  50.5 0.1 copy.98
  50.6 0.1 copy.96
  50.7 0.3 fusion.84
  51.0 0.1 copy.94
  51.1 0.1 copy.92
  51.2 2.7 %gather_fusion.1 = bf16[2,4,2,3,2,2048]{5,4,3,2,1,0:T(2,128)(2,1)S(1)} fusion(bf16[4,8,2,3,2,2048]{5,4,3,2,1,0:T(2,128)(2,1)} %all-gather.2.cloned.1.call-done, s32[1024]{0:T(1024)S(1)} %get-tuple-element.23), kind=kCustom, calls=%fused_computation.1 | custom fusion | bytes 786440 | tf_op jit(solution)/shard_map/gather | solution.py:42
  54.0 0.4 fusion.29
  54.4 0.3 fusion.83
  54.7 0.1 copy.97
  54.8 0.1 copy.95
  54.9 0.3 fusion.85
  55.2 0.1 copy.93
  55.3 0.1 copy.91
  55.4 0.6 fusion.24
  56.0 0.9 %convert_reduce_fusion = f32[2,3,3,2,2048]{4,3,2,1,0:T(2,128)S(1)} fusion(bf16[4,2,1,1,3,3,1,2048]{7,0,6,5,4,3,2,1:T(4,128)(2,1)S(1)} %get-tuple-element.10, bf16[4,2,1,1,3,3,1,2048]{7,0,6,5,4,3,2,1:T(4,128)(2,1)S(1)} %get-tuple-element.9), kind=kLoop, calls=%fused_computation.21 | loop fusion | flops 811008 | bytes 884736 | tf_op jit(solution)/shard_map/reduce_sum | solution.py:118
  56.9 0.2 fusion.26
  57.1 0.6 slice_reduce_fusion
  57.7 0.2 reshape_squeeze.6
  57.9 0.5 fusion.36
  58.4 0.5 fusion.40
  58.9 0.2 reshape_squeeze.7
  59.1 0.5 convolution_add_fusion
  59.6 0.3 copy.76
  59.9 0.5 convolution_subtract_fusion
  60.4 0.3 copy.75
  60.7 10.9 %fusion.3 = f32[64,64,18]{1,2,0:T(8,128)S(1)} fusion(f32[18,64,64]{1,0,2:T(8,128)S(1)} %copy.76, s32[64,64]{0,1:T(8,128)S(1)} %add_add_fusion), kind=kOutput, calls=%fused_computation.8 | convolution fusion | flops 60293120 | bytes 606208 | tf_op jit(solution)/shard_map/rfp,fqp->rqp/dot_general | solution.py:100
  71.6 10.7 %fusion.19 = bf16[18,64,64]{1,0,2:T(8,128)(2,1)S(1)} fusion(f32[64,64,18]{1,2,0:T(8,128)S(1)} %fusion.3, f32[18,64,64]{1,0,2:T(8,128)S(1)} %copy.75, s32[64,64]{0,1:T(8,128)S(1)} %add_add_fusion), kind=kOutput, calls=%fused_computation.20 | convolution fusion | flops 60514304 | bytes 753664 | tf_op jit(solution)/shard_map/rfp,fqp->rqp/dot_general | solution.py:100
  82.3 0.3 copy.77
  82.6 0.2 convert_element_type.155
  82.8 0.8 copy.78
  (12 shorter events, 0.2 us)
Async XLA Ops:
  6.5 15.7 %copy-start = (s32[1,8,2]{1,2,0:T(2,128)S(1)}, s32[1,8,2]{1,2,0:T(2,128)}, u32[]{:S(2)}) copy-start(s32[1,8,2]{1,2,0:T(2,128)} %param.4) | copy-start | bytes 196
  6.5 4.1 %copy-start.1 = (bf16[1,1,2,3,2,2048]{5,4,3,2,1,0:T(2,128)(2,1)S(1)}, bf16[1,1,2,3,2,2048]{5,4,3,2,1,0:T(2,128)(2,1)}, u32[]{:S(2)}) copy-start(bf16[1,1,2,3,2,2048]{5,4,3,2,1,0:T(2,128)(2,1)} %param.3) | copy-start | bytes 147460
  6.5 40.5 %all-gather.2.cloned.1.call-start = ((), (), s32[]{:S(2)}) async-start(), calls=%async_computation | async-start | bytes 1769472 | tf_op jit(solution)/shard_map/all_gather | solution.py:114
Sparse Core Ops, SparseCore 0:
  21.7 25.3 all-gather.1
where the time goes:
time: 90.8 us; the launch traced here: 90.5 us
  waiting for transfers between devices  24.3 us (27%)
  matrix products  23.5 us (26%)
  between operations  14.4 us (16%)
  local copies, waits for them, and re-layouts  11.3 us (12%)
  blocking collectives  10.9 us (12%)
  other arithmetic  6.17 us (7%)
    all_gather x1, waiting for transfers between devices, body(): every = lax.all_gather(local_hours, 'sta', axis=1, tiled=True)  24.3 us
    all_gather x1, blocking collectives, body(): local_hours = lax.all_gather(white, 'tm', axis=0, tiled=True)  10.9 us
    dot_general x1, matrix products, lag_values(): jnp.einsum(form_second, middle_im, sin_second, precision=high)  10.9 us
    dot_general x1, matrix products, lag_values(): jnp.einsum(form_second, middle_re, cos_second, precision=high)  10.7 us
    gather x1, local copies, waits for them, and re-layouts, cross_hours(): right = grouped[:, chosen[:, 1]]  2.75 us
    gather x1, local copies, waits for them, and re-layouts, cross_hours(): left = grouped[:, chosen[:, 0]]  2.74 us
    another operation x3, other arithmetic  2.16 us
  transfers between devices with their start and end apart: 1, of which 1 were waited for; matrix products, arithmetic and copies ran while one was open for 1% of the time, Pallas kernels for 0%

commit v1 on v0

v1 whole, which is shorter than its diff:
```python
import functools
import math

import jax
import jax.numpy as jnp
import numpy as np
from jax import lax
from jax.experimental import pallas as pl
from jax.experimental.pallas import tpu as pltpu
from jax.sharding import PartitionSpec as P

SMOOTH = 64
LANES = 128
PARTS = 3
SLAB = 8

epsilon = 1e-05
MESH_AXES = ("tm", "sta")
VMEM = pl.BlockSpec(memory_space=pltpu.VMEM)


def kernel_call(kernel, out_shape, operands, scratch):
    return pl.pallas_call(
        kernel,
        out_shape=out_shape,
        in_specs=[VMEM] * operands,
        out_specs=VMEM,
        scratch_shapes=scratch,
        compiler_params=pltpu.CompilerParams(vmem_limit_bytes=40 * 1024 * 1024),
    )


def whiten_kernel(segments, owners, x_ref, o_ref, rows):
    shards, _, width = x_ref.shape
    run = width // segments
    reach = SMOOTH // shards
    lane = lax.broadcasted_iota(jnp.int32, (SLAB, width), 1) % run

    def moved(value, step):
        inside = (lane + step >= 0) & (lane + step < run)
        return jnp.where(inside, pltpu.roll(value, (-step) % width, 1), 0.0)

    values, sizes = [], []
    for d in range(shards):
        value = x_ref[d].astype(jnp.float32)
        square = value * value
        values.append(value)
        sizes.append(jnp.sqrt(square + pltpu.roll(square, 4, 0)))
    upto, beyond = [sizes[0]], [sizes[-1]]
    for d in range(1, shards):
        upto.append(upto[-1] + sizes[d])
        beyond.append(beyond[-1] + sizes[shards - 1 - d])
    beyond = beyond[::-1]
    middle = upto[-1]
    for step in range(1, reach):
        middle = middle + (moved(upto[-1], step) + moved(upto[-1], -step))
    bins = run * shards
    for d in range(shards):
        window = middle + (moved(beyond[d], -reach) + moved(upto[d], reach))
        place = lane * shards + d
        count = jnp.minimum(place + SMOOTH, bins - 1) - jnp.maximum(place - SMOOTH, 0) + 1
        smoothed = window / count.astype(jnp.float32)
        white = values[d] / (smoothed + epsilon)
        for v in range(width // LANES):
            for c in range(2):
                first = (v * 2 + c) * PARTS
                rows[d, first : first + PARTS] = white[c * 4 : c * 4 + PARTS, v * LANES : (v + 1) * LANES]
    packed = rows[...].astype(jnp.bfloat16)
    for device, d in enumerate(owners):
        o_ref[device] = packed[d]


def cross_kernel(segments, share, pick_ref, w_ref, o_ref, rows):
    hours, depth, _ = w_ref.shape
    slots = pick_ref.shape[1]
    group = slots // share
    chunk = o_ref.shape[1]
    kinds = 2 * PARTS
    halves = chunk // (share * PARTS * PARTS * 2)
    blocks = segments * halves * kinds
    column = lax.broadcasted_iota(jnp.int32, (slots, depth), 1)
    sides = []
    for side in range(2):
        offset = column - pick_ref[side]
        sides.append([(offset == r).astype(jnp.bfloat16) for r in range(blocks)])
    chosen = jnp.concatenate(sides[0] + sides[1], axis=0)
    picked = [
        jnp.dot(chosen, w_ref[h], preferred_element_type=jnp.float32) for h in range(hours)
    ]

    def part(side, h, g, j, c, x):
        first = (side * blocks + ((g * halves + j) * 2 + c) * PARTS + x) * slots
        return picked[h][first : first + slots]

    for j in range(halves):
        real = [None] * (PARTS * PARTS)
        imag = [None] * (PARTS * PARTS)
        for h in range(hours):
            for g in range(segments):
                left = [[part(0, h, g, j, c, x) for x in range(PARTS)] for c in range(2)]
                right = [[part(1, h, g, j, c, x) for x in range(PARTS)] for c in range(2)]
                for x in range(PARTS):
                    for y in range(PARTS):
                        re = left[0][x] * right[0][y] + left[1][x] * right[1][y]
                        im = left[0][x] * right[1][y] - left[1][x] * right[0][y]
                        n = x * PARTS + y
                        real[n] = re if real[n] is None else real[n] + re
                        imag[n] = im if imag[n] is None else imag[n] + im
        for n in range(PARTS * PARTS):
            for c, total in enumerate((real[n], imag[n])):
                for u in range(share):
                    row = ((u * PARTS * PARTS + n) * 2 + c) * halves + j
                    rows[pl.ds(row, group, stride=chunk), :] = total[u * group : (u + 1) * group]
    o_ref[...] = rows[...].reshape(o_ref.shape).astype(jnp.bfloat16)


def lag_kernel(live_ref, d_ref, first_ref, cos_ref, sin_ref, second_ref, o_ref, rows):
    lines, period = cos_ref.shape
    pieces = d_ref.shape[0] // lines
    share = o_ref.shape[0]
    rows[...] = d_ref[...].astype(jnp.float32)
    daily = jnp.concatenate(
        [rows[pl.ds(k, lines, stride=pieces), :].astype(jnp.bfloat16) for k in range(pieces)], axis=1
    )
    middle = jnp.dot(daily, first_ref[...], preferred_element_type=jnp.float32)
    re, im = middle[:, :period], middle[:, period:]
    turned = jnp.concatenate(
        [
            (re * cos_ref[...] - im * sin_ref[...]).astype(jnp.bfloat16),
            (re * sin_ref[...] + im * cos_ref[...]).astype(jnp.bfloat16),
        ],
        axis=0,
    )
    joined = jnp.dot(second_ref[...], turned, preferred_element_type=jnp.float32)
    turns = joined.shape[0] // (share * PARTS * SLAB)
    for a in range(turns):
        for u in range(share):
            for x in range(PARTS):
                first = ((a * share + u) * PARTS + x) * SLAB
                value = jnp.where(live_ref[u] > 0, joined[first : first + PARTS], 0.0)
                o_ref[u, x, :, a * period : (a + 1) * period] = value.astype(jnp.bfloat16)


def lag_tables(bins, shards, share):
    lags = 2 * bins
    period = lags // shards
    per_slot = PARTS * PARTS
    k = np.arange(bins // shards)[:, None]
    b = np.arange(period)[None, :]
    angle = (k * b % period) * (2.0 * math.pi / period)
    cos, sin = np.cos(angle), np.sin(angle)
    first = np.block([[cos, sin], [-sin, cos]])
    d = np.arange(shards)[:, None]
    angle = np.repeat(d * b * (2.0 * math.pi / lags), share * per_slot, axis=0)
    scale = bins**-0.5
    a = np.arange(shards)[:, None] - bins // period
    turn = (a * d.T % shards) * (2.0 * math.pi / shards)
    line = np.eye(share * per_slot).reshape(share, PARTS, PARTS, -1)
    line = np.pad(line, ((0, 0), (0, 0), (0, SLAB - PARTS), (0, 0))).reshape(-1, share * per_slot)
    second = [
        np.einsum("ad,mr->amdr", table, line).reshape(shards * line.shape[0], -1)
        for table in (np.cos(turn), -np.sin(turn))
    ]
    return (
        jnp.asarray(first, jnp.bfloat16),
        jnp.asarray(np.cos(angle) * scale, jnp.float32),
        jnp.asarray(np.sin(angle) * scale, jnp.float32),
        jnp.asarray(np.concatenate(second, axis=1), jnp.bfloat16),
    )


def body(spectra, pair_blocks, block_count):
    _, _, segments, parts, _, bins = spectra.shape
    slots = pair_blocks.shape[1]
    hours, stations = lax.axis_size("tm"), lax.axis_size("sta")
    near = 2
    shards = hours * near
    share = slots // hours
    run = bins // shards
    halves = run // LANES
    chunk_in = segments * halves * 2 * parts
    chunk_out = share * parts * parts * 2 * halves

    def shard(t, s):
        return t * near + s % near

    swap = [(s, s ^ 1) for s in range(stations)]
    other = lax.ppermute(pair_blocks, "sta", swap)
    is_second = lax.axis_index("sta") % near == 1
    both = jnp.where(is_second, jnp.concatenate([other, pair_blocks]), jnp.concatenate([pair_blocks, other]))
    lists = both.reshape(near, hours, share, 2).transpose(3, 2, 1, 0).reshape(2, share * shards, 1)
    depth = stations * chunk_in
    pick = jnp.broadcast_to(lists * chunk_in, (2, share * shards, depth))

    strided = spectra[0, 0].reshape(segments, parts, 2, run, shards).transpose(4, 2, 1, 0, 3)
    strided = jnp.pad(strided, ((0, 0), (0, 0), (0, 1), (0, 0), (0, 0)))
    strided = strided.reshape(shards, SLAB, segments * run)

    owners = [shard(t, s) for t in range(hours) for s in range(stations)]
    white = kernel_call(
        functools.partial(whiten_kernel, segments, owners),
        jax.ShapeDtypeStruct((hours * stations, chunk_in, LANES), jnp.bfloat16),
        1,
        [pltpu.VMEM((shards, chunk_in, LANES), jnp.float32)],
    )(strided)
    every = lax.all_to_all(white, MESH_AXES, 0, 0, tiled=True)

    daily = kernel_call(
        functools.partial(cross_kernel, segments, share),
        jax.ShapeDtypeStruct((shards, chunk_out, LANES), jnp.bfloat16),
        2,
        [pltpu.VMEM((shards * chunk_out, LANES), jnp.float32)],
    )(pick, every.reshape(hours, depth, LANES))

    groups = [
        [t * stations + s + e for t in range(hours) for e in range(near)] for s in range(0, stations, near)
    ]
    mine = lax.all_to_all(daily, MESH_AXES, 0, 0, tiled=True, axis_index_groups=groups)

    first_slot = lax.axis_index("tm") * share
    live = (first_slot + jnp.arange(share, dtype=jnp.int32) < block_count[0]).astype(jnp.int32)
    result = pl.pallas_call(
        lag_kernel,
        out_shape=jax.ShapeDtypeStruct((share, parts, parts, 2 * bins), jnp.bfloat16),
        in_specs=[pl.BlockSpec(memory_space=pltpu.SMEM)] + [VMEM] * 5,
        out_specs=VMEM,
        scratch_shapes=[pltpu.VMEM((shards * chunk_out, LANES), jnp.float32)],
        compiler_params=pltpu.CompilerParams(vmem_limit_bytes=40 * 1024 * 1024),
    )(live, mine.reshape(shards * chunk_out, LANES), *lag_tables(bins, shards, share))
    return result.reshape(1, share, 1, 1, parts, parts, 2 * bins)


def solution(mesh):
    placed = (P("tm", "sta", None, None, None, None), P("sta", None, None), P("sta"))
    return jax.shard_map(
        body,
        mesh=mesh,
        in_specs=placed,
        out_specs=P("sta", "tm", None, None, None, None, None),
        check_vma=False,
    )
```

time: 90.8 us -> 32.1 us (0.35)
  matrix products: 23.5 us -> 0 us
  between operations: 14.4 us -> 0.76 us
  waiting for transfers between devices: 24.3 us -> 13 us
  starting transfers between devices: 0.01 us -> 11 us
  blocking collectives: 10.9 us -> 0 us
  local copies, waits for them, and re-layouts: 11.3 us -> 3.39 us
  other arithmetic: 6.17 us -> 0.01 us
  Pallas kernels: 0 us -> 3.62 us
    all_gather x1 -> x0, waiting for transfers between devices: 24.3 us -> none  [body(): every = lax.all_gather(local_hours, 'sta', axis=1, tiled=True)]
    dot_general x6 -> x0, matrix products: 23.5 us -> none  [the longest x1 10.9 us: lag_values(): jnp.einsum(form_second, middle_im, sin_second, precision=high)]
    all_to_all x0 -> x2, waiting for transfers between devices: none -> 12.2 us  [the longest x1 7.22 us: body(): every = lax.all_to_all(white, MESH_AXES, 0, 0, tiled=True)]
    all_gather x1 -> x0, blocking collectives: 10.9 us -> none  [body(): local_hours = lax.all_gather(white, 'tm', axis=0, tiled=True)]
    all_to_all x0 -> x2, starting transfers between devices: none -> 10.7 us  [the longest x1 7.3 us: body(): every = lax.all_to_all(white, MESH_AXES, 0, 0, tiled=True)]
    gather x2 -> x0, local copies, waits for them, and re-layouts: 5.49 us -> none  [the longest x1 2.75 us: cross_hours(): right = grouped[:, chosen[:, 1]]]
    pallas_call x0 -> x3, Pallas kernels: none -> 3.62 us  [the longest x1 1.41 us: body(): kernel_call(functools.partial(cross_kernel, segments, share), jax.ShapeDt...]
    another operation x4 -> x0, other arithmetic: 2.78 us -> none
  transfers between devices with their start and end apart: 1 -> 3, of which waited for: 1 -> 3; matrix products, arithmetic and copies ran while one was open for 1% -> 1% of each run, Pallas kernels for 0% -> 0%
where the time goes in v1:
time: 32.1 us; the launch traced here: 31.8 us
  waiting for transfers between devices  13 us (40%)
  starting transfers between devices  11 us (34%)
  Pallas kernels  3.62 us (11%)
  local copies, waits for them, and re-layouts  3.39 us (11%)
  between operations  0.76 us (2%)
    all_to_all x1, starting transfers between devices, body(): every = lax.all_to_all(white, MESH_AXES, 0, 0, tiled=True)  7.3 us
    all_to_all x1, waiting for transfers between devices, body(): every = lax.all_to_all(white, MESH_AXES, 0, 0, tiled=True)  7.22 us
    all_to_all x1, waiting for transfers between devices, body(): lax.all_to_all(daily, MESH_AXES, 0, 0, tiled=True, axis_index_groups=groups)  4.97 us
    all_to_all x1, starting transfers between devices, body(): lax.all_to_all(daily, MESH_AXES, 0, 0, tiled=True, axis_index_groups=groups)  3.38 us
    another operation x1, local copies, waits for them, and re-layouts, body(): spectra[0, 0].reshape(segments, parts, 2, run, shards)  1.71 us
    pallas_call x1, Pallas kernels, body(): kernel_call(functools.partial(cross_kernel, segments, share), jax.ShapeDt...  1.41 us
    pallas_call x1, Pallas kernels, body(): pl.pallas_call(lag_kernel, out_shape=jax.ShapeDtypeStruct((share, parts,...  1.25 us
    pallas_call x1, Pallas kernels, body(): kernel_call(functools.partial(whiten_kernel, segments, owners), jax.Shape...  0.96 us
  transfers between devices with their start and end apart: 3, of which 3 were waited for; matrix products, arithmetic and copies ran while one was open for 1% of the time, Pallas kernels for 0%

profile of v1, /device:TPU:0, one launch (start us, length us, event | category | flops | bytes accessed | tf_op | source)
XLA Modules:
  0.0 31.8 jit_solution(2942250655858166448)
XLA Ops:
  0.0 1.7 %reshape_squeeze.3 = bf16[2,3,2,256,8]{4,3,2,1,0:T(8,128)(2,1)S(1)} reshape(bf16[1,1,2,3,2,2048]{5,4,3,2,1,0:T(2,128)(2,1)} %param.7) | data formatting | bytes 98304 | tf_op jit(solution)/shard_map/reshape;squeeze | solution.py:195
  1.7 0.0 copy-start.4
  1.7 0.0 copy-start.3
  1.7 0.3 copy.14
  2.0 0.0 copy-start
  2.1 1.0 %shard_map.73 = bf16[32,24,128]{2,1,0:T(8,128)(2,1)} custom-call(bf16[8,8,512]{2,1,0:T(8,128)(2,1)S(1)} %reshape.27.x_ref), custom_call_target="tpu_custom_call" | custom-call | tf_op jit(solution)/shard_map/pallas_call | solution.py:200
  3.1 7.3 %all-to-all-start = ((bf16[32,24,128]{2,1,0:T(8,128)(2,1)}), bf16[32,24,128]{2,1,0:T(8,128)(2,1)S(1)}, u32[]{:S(2)}, u32[]{:S(2)}) async-start(bf16[32,24,128]{2,1,0:T(8,128)(2,1)} %shard_map.73), calls=%async_computation | async-start | bytes 393216 | tf_op jit(solution)/shard_map/all_to_all | solution.py:206
  10.4 0.0 copy-done.4
  10.4 0.3 collective-permute-start
  10.7 0.1 concatenate.13
  10.8 0.8 %collective-permute-done = s32[1,8,2]{1,2,0:T(2,128)S(1)} collective-permute-done((s32[1,8,2]{1,2,0:T(2,128)S(1)}, s32[1,8,2]{1,2,0:T(2,128)S(1)}, u32[]{:S(2)}, u32[]{:S(2)}) %collective-permute-start) | collective-permute-done | bytes 96 | tf_op jit(solution)/shard_map/ppermute | solution.py:188
  11.6 0.1 concatenate.12
  11.7 0.1 copy.11
  11.8 0.1 mul.24
  11.9 7.2 %all-to-all-done = bf16[32,24,128]{2,1,0:T(8,128)(2,1)S(1)} async-done(((bf16[32,24,128]{2,1,0:T(8,128)(2,1)}), bf16[32,24,128]{2,1,0:T(8,128)(2,1)S(1)}, u32[]{:S(2)}, u32[]{:S(2)}) %all-to-all-start) | async-done | bytes 196640 | tf_op jit(solution)/shard_map/all_to_all | solution.py:206
  19.1 0.1 broadcast_in_dim.2.pick_ref
  19.2 0.0 copy-start.1
  19.2 0.0 copy-start.2
  19.2 1.4 %shard_map.74 = bf16[8,72,128]{2,1,0:T(8,128)(2,1)} custom-call(s32[2,16,192]{2,1,0:T(8,128)S(1)} %broadcast_in_dim.2.pick_ref, bf16[4,192,128]{2,1,0:T(8,128)(2,1)S(1)} %bitcast.12), custom_call_target="tpu_custom_call" | custom-call | tf_op jit(solution)/shard_map/pallas_call | solution.py:208
  20.6 3.4 %all-to-all-start.1 = ((bf16[8,72,128]{2,1,0:T(8,128)(2,1)}), bf16[8,72,128]{2,1,0:T(8,128)(2,1)S(1)}, u32[]{:S(2)}, u32[]{:S(2)}) async-start(bf16[8,72,128]{2,1,0:T(8,128)(2,1)} %shard_map.74), calls=%async_computation.1 | async-start | bytes 294912 | tf_op jit(solution)/shard_map/all_to_all | solution.py:218
  24.7 5.0 %all-to-all-done.1 = bf16[8,72,128]{2,1,0:T(8,128)(2,1)S(1)} async-done(((bf16[8,72,128]{2,1,0:T(8,128)(2,1)}), bf16[8,72,128]{2,1,0:T(8,128)(2,1)S(1)}, u32[]{:S(2)}, u32[]{:S(2)}) %all-to-all-start.1) | async-done | bytes 147488 | tf_op jit(solution)/shard_map/all_to_all | solution.py:218
  29.6 0.0 copy-done.3
  29.7 0.0 copy-done
  29.7 0.0 copy-done.1
  29.7 0.0 copy-done.2
  29.7 1.2 %shard_map.75 = bf16[2,3,3,4096]{3,2,1,0:T(4,128)(2,1)S(1)} custom-call(s32[2]{0:T(128)S(1)} %compare_convert_fusion.live_ref, bf16[576,128]{1,0:T(8,128)(2,1)S(1)} %bitcast.14, bf16[512,1024]{1,0:T(8,128)(2,1)S(1)} %copy-done, f32[144,512]{1,0:T(8,128)S(1)} %copy-done.3, f32[144,512]{1,0:T(8,128)S(1)} %copy-done.2, bf16[384,288]{1,0:T(8,128)(2,1)S(1)} %copy-done.1), custom_call_target="tpu_custom_call" | custom-call | tf_op jit(solution)/shard_map/pallas_call | solution.py:222
  30.9 0.8 %copy.13 = bf16[1,2,1,1,3,3,4096]{6,1,5,4,3,2,0:T(2,128)(2,1)} copy(bf16[1,2,1,1,3,3,4096]{6,5,4,1,3,2,0:T(4,128)(2,1)S(1)} %bitcast.13) | data formatting | bytes 294912 | tf_op jit(solution)/shard_map/reshape | solution.py:230
  (4 shorter events, 0.1 us)
Async XLA Ops:
  1.7 8.7 %copy-start.4 = (s32[1,8,2]{1,2,0:T(2,128)S(1)}, s32[1,8,2]{1,2,0:T(2,128)}, u32[]{:S(2)}) copy-start(s32[1,8,2]{1,2,0:T(2,128)} %param.8) | copy-start | bytes 196
  1.7 27.9 %copy-start.3 = (f32[144,512]{1,0:T(8,128)S(1)}, f32[144,512]{1,0:T(8,128)}, u32[]{:S(2)}) copy-start(f32[144,512]{1,0:T(8,128)} %constant.36.clone.cos_ref) | copy-start | bytes 884740
  2.0 27.6 %copy-start = (bf16[512,1024]{1,0:T(8,128)(2,1)S(1)}, bf16[512,1024]{1,0:T(8,128)(2,1)}, u32[]{:S(2)}) copy-start(bf16[512,1024]{1,0:T(8,128)(2,1)} %constant.35.clone.first_ref) | copy-start | bytes 3145732
  3.1 16.1 %all-to-all-start = ((bf16[32,24,128]{2,1,0:T(8,128)(2,1)}), bf16[32,24,128]{2,1,0:T(8,128)(2,1)S(1)}, u32[]{:S(2)}, u32[]{:S(2)}) async-start(bf16[32,24,128]{2,1,0:T(8,128)(2,1)} %shard_map.73), calls=%async_computation | async-start | bytes 393216 | tf_op jit(solution)/shard_map/all_to_all | solution.py:206
  10.4 1.2 %collective-permute-start = (s32[1,8,2]{1,2,0:T(2,128)S(1)}, s32[1,8,2]{1,2,0:T(2,128)S(1)}, u32[]{:S(2)}, u32[]{:S(2)}) collective-permute-start(s32[1,8,2]{1,2,0:T(2,128)S(1)} %copy-done.4), channel_id=1, source_target_pairs={{0,1},{1,0},{2,3},{3,2},{4,5},{5,4},{6,7},{7,6},{8,9},{9,8},{10,11... | collective-permute-start | bytes 200 | tf_op jit(solution)/shard_map/ppermute | solution.py:188
  19.2 10.4 %copy-start.1 = (bf16[384,288]{1,0:T(8,128)(2,1)S(1)}, bf16[384,288]{1,0:T(8,128)(2,1)}, u32[]{:S(2)}) copy-start(bf16[384,288]{1,0:T(8,128)(2,1)} %constant.38.clone.second_ref) | copy-start | bytes 663556
  19.2 10.4 %copy-start.2 = (f32[144,512]{1,0:T(8,128)S(1)}, f32[144,512]{1,0:T(8,128)}, u32[]{:S(2)}) copy-start(f32[144,512]{1,0:T(8,128)} %constant.37.clone.sin_ref) | copy-start | bytes 884740
  20.6 9.0 %all-to-all-start.1 = ((bf16[8,72,128]{2,1,0:T(8,128)(2,1)}), bf16[8,72,128]{2,1,0:T(8,128)(2,1)S(1)}, u32[]{:S(2)}, u32[]{:S(2)}) async-start(bf16[8,72,128]{2,1,0:T(8,128)(2,1)} %shard_map.74), calls=%async_computation.1 | async-start | bytes 294912 | tf_op jit(solution)/shard_map/all_to_all | solution.py:218

commit v2 on v1

v2 whole, which is shorter than its diff:
```python
import functools
import math

import jax
import jax.numpy as jnp
import numpy as np
from jax import lax
from jax.experimental import pallas as pl
from jax.experimental.pallas import tpu as pltpu
from jax.sharding import PartitionSpec as P

SMOOTH = 64
LANES = 128
PARTS = 3
SLAB = 8

epsilon = 1e-05
MESH_AXES = ("tm", "sta")
VMEM = pl.BlockSpec(memory_space=pltpu.VMEM)
HBM = pl.BlockSpec(memory_space=pltpu.HBM)


def in_hbm(array):
    return pltpu.with_memory_space_constraint(array, pltpu.HBM)


def kernel_call(kernel, out_shape, in_specs, scratch):
    return pl.pallas_call(
        kernel,
        out_shape=out_shape,
        in_specs=in_specs,
        out_specs=jax.tree.map(lambda _: VMEM, out_shape),
        scratch_shapes=scratch,
        compiler_params=pltpu.CompilerParams(vmem_limit_bytes=40 * 1024 * 1024),
    )


def whiten_kernel(
    owners, shards, segments, spectra_ref, pairs_ref, count_ref, o_ref, mine_ref, live_ref, x_ref, rows, sems
):
    bins = x_ref.shape[2]
    tiles = bins // LANES
    copies = [
        pltpu.make_async_copy(source, target, sems.at[n])
        for n, (source, target) in enumerate(((spectra_ref, x_ref), (pairs_ref, mine_ref)))
    ]
    for copy in copies:
        copy.start()
    lane = lax.broadcasted_iota(jnp.int32, (SLAB, LANES), 1)
    even = lax.broadcasted_iota(jnp.int32, (SLAB, LANES), 0) % 2 == 0
    turn = [lane % shards == k for k in range(shards)]
    blank = jnp.zeros((SLAB, LANES), jnp.float32)
    apart = lax.broadcasted_iota(jnp.int32, (3 * LANES, LANES), 0) - LANES
    apart = apart - lax.broadcasted_iota(jnp.int32, (3 * LANES, LANES), 1)
    band = (jnp.abs(apart) <= SMOOTH).astype(jnp.bfloat16)
    copies[0].wait()
    values, blocks = [], []
    for g in range(segments):
        lines = [x_ref[g * PARTS + x].astype(jnp.float32) for x in range(PARTS)]
        lines = jnp.concatenate(lines + [jnp.zeros((SLAB - 2 * PARTS, bins), jnp.float32)], axis=0)
        value = [lines[:, v * LANES : (v + 1) * LANES] for v in range(tiles)]
        size = [blank]
        for v in range(tiles):
            square = value[v] * value[v]
            twin = jnp.where(even, pltpu.roll(square, SLAB - 1, 0), pltpu.roll(square, 1, 0))
            size.append(jnp.sqrt(square + twin))
        size.append(blank)
        values.append(value)
        blocks += [jnp.concatenate(size[v : v + 3], axis=1) for v in range(tiles)]
    stacked = jnp.concatenate(blocks, axis=0)
    high = stacked.astype(jnp.bfloat16)
    low = (stacked - high.astype(jnp.float32)).astype(jnp.bfloat16)
    window = jnp.dot(high, band, preferred_element_type=jnp.float32) + jnp.dot(
        low, band, preferred_element_type=jnp.float32
    )
    halves = tiles // shards
    for g in range(segments):
        for j in range(halves):
            moved = []
            for i in range(shards):
                v = j * shards + i
                place = lane + v * LANES
                count = jnp.minimum(place + SMOOTH, bins - 1) - jnp.maximum(place - SMOOTH, 0) + 1
                first = (g * tiles + v) * SLAB
                smoothed = window[first : first + SLAB] / count.astype(jnp.float32)
                white = values[g][v] / (smoothed + epsilon)
                moved.append(pltpu.roll(white, i, 1) if i else white)
            first = (g * halves + j) * 2 * PARTS
            for d in range(shards):
                mixed = moved[0]
                for i in range(1, shards):
                    mixed = jnp.where(turn[(d + i) % shards], moved[i], mixed)
                if d:
                    mixed = pltpu.roll(mixed, LANES - d, 1)
                rows[d, first : first + 2 * PARTS] = mixed[: 2 * PARTS]
    packed = rows[...].astype(jnp.bfloat16)
    for device, d in enumerate(owners):
        o_ref[device] = packed[d]
    copies[1].wait()
    live_ref[...] = jnp.full(live_ref.shape, count_ref[0])


def station_columns(pair_refs, hours, share):
    near = len(pair_refs)
    rows = share * hours * near
    lane = lax.broadcasted_iota(jnp.int32, (rows, hours * share), 1)
    row = lax.broadcasted_iota(jnp.int32, (rows, hours * share), 0)
    owner = row % near
    slot = row // near % hours * share + row // (near * hours)
    second = lax.axis_index("sta") % near == 1
    columns = []
    for side in range(2):
        mine, other = [jnp.broadcast_to(ref[side : side + 1], lane.shape) for ref in pair_refs]
        lists = [jnp.where(second, other, mine), jnp.where(second, mine, other)]
        value = jnp.where(owner == 1, lists[1], lists[0])
        columns.append(jnp.sum(jnp.where(lane == slot, value, 0), axis=1, keepdims=True))
    return columns


def cross_kernel(segments, share, mine_ref, other_ref, w_ref, table_ref, o_ref, held_ref, rows, sem):
    hours, depth, _ = w_ref.shape
    table_copy = pltpu.make_async_copy(table_ref, held_ref, sem)
    table_copy.start()
    group, chunk, _ = o_ref.shape
    slots = group * share
    kinds = 2 * PARTS
    halves = chunk // (share * PARTS * PARTS * 2)
    blocks = segments * halves * kinds
    column = lax.broadcasted_iota(jnp.int32, (slots, depth), 1)
    sides = []
    for station in station_columns((mine_ref, other_ref), hours, share):
        offset = column - station * blocks
        sides.append([(offset == r).astype(jnp.bfloat16) for r in range(blocks)])
    chosen = jnp.concatenate(sides[0] + sides[1], axis=0)
    picked = [
        jnp.dot(chosen, w_ref[h], preferred_element_type=jnp.float32) for h in range(hours)
    ]

    def part(side, h, g, j, c, x):
        first = (side * blocks + ((g * halves + j) * PARTS + x) * 2 + c) * slots
        return picked[h][first : first + slots]

    for j in range(halves):
        real = [None] * (PARTS * PARTS)
        imag = [None] * (PARTS * PARTS)
        for h in range(hours):
            for g in range(segments):
                left = [[part(0, h, g, j, c, x) for x in range(PARTS)] for c in range(2)]
                right = [[part(1, h, g, j, c, x) for x in range(PARTS)] for c in range(2)]
                for x in range(PARTS):
                    for y in range(PARTS):
                        re = left[0][x] * right[0][y] + left[1][x] * right[1][y]
                        im = left[0][x] * right[1][y] - left[1][x] * right[0][y]
                        n = x * PARTS + y
                        real[n] = re if real[n] is None else real[n] + re
                        imag[n] = im if imag[n] is None else imag[n] + im
        for n in range(PARTS * PARTS):
            for c, total in enumerate((real[n], imag[n])):
                for u in range(share):
                    row = ((u * PARTS * PARTS + n) * 2 + c) * halves + j
                    rows[pl.ds(row, group, stride=chunk), :] = total[u * group : (u + 1) * group]
    o_ref[...] = rows[...].reshape(o_ref.shape).astype(jnp.bfloat16)
    table_copy.wait()


def lag_kernel(live_ref, d_ref, table_ref, o_ref, rows):
    share, lags = o_ref.shape[2:]
    shards = lax.axis_size("tm") * 2
    period = lags // shards
    pieces = period // LANES
    lines = d_ref.shape[0] // (pieces * shards)
    total = lines * shards
    rows[...] = d_ref[...].astype(jnp.float32)
    daily = []
    for k in range(pieces):
        column = [rows[pl.ds(r * pieces + k, shards, stride=lines * pieces), :] for r in range(lines)]
        daily.append(jnp.concatenate(column, axis=0).astype(jnp.bfloat16))
    daily = jnp.concatenate(daily, axis=1)
    middle = jnp.dot(daily, table_ref[:period, : 2 * period], preferred_element_type=jnp.float32)
    middle = middle.reshape(lines, shards, 2 * period)
    re, im = middle[:, :, :period], middle[:, :, period:]
    turn = table_ref[period + total : period + total + 2 * shards, : 2 * period].astype(jnp.float32)
    turn = turn[:shards] + turn[shards:]
    cos, sin = turn[None, :, :period], turn[None, :, period:]
    turned = jnp.concatenate(
        [
            (re * cos - im * sin).reshape(total, period).astype(jnp.bfloat16),
            (re * sin + im * cos).reshape(total, period).astype(jnp.bfloat16),
        ],
        axis=0,
    )
    second = table_ref[period : period + total, : 2 * total]
    joined = jnp.dot(second, turned, preferred_element_type=jnp.float32)
    live = live_ref[:1, :1] - lax.axis_index("tm") * share
    slot = lax.broadcasted_iota(jnp.int32, joined.shape, 0) % share
    joined = jnp.where(slot < live, joined, 0.0)
    for a in range(shards):
        for n in range(PARTS * PARTS):
            first = (a * PARTS * PARTS + n) * share
            value = joined[first : first + share].astype(jnp.bfloat16)
            o_ref[n // PARTS, n % PARTS, :, a * period : (a + 1) * period] = value


def lag_table(bins, shards, share):
    lags = 2 * bins
    period = lags // shards
    lines = share * PARTS * PARTS
    lane = np.arange(LANES)
    inner = lane % shards * (LANES // shards) + lane // shards
    k = (np.arange(0, bins // shards, LANES)[:, None] + inner).reshape(-1, 1)
    b = np.arange(period)[None, :]
    angle = (k * b % period) * (2.0 * math.pi / period)
    cos, sin = np.cos(angle), np.sin(angle)
    first = np.block([[cos, sin], [-sin, cos]])
    d = np.arange(shards)[:, None]
    a = np.arange(shards)[:, None] - bins // period
    turn = (a * d.T % shards) * (2.0 * math.pi / shards)
    same = np.eye(lines).reshape(share, PARTS * PARTS, lines).transpose(1, 0, 2)
    second = [np.einsum("ad,nur->anurd", table, same) for table in (np.cos(turn), -np.sin(turn))]
    second = np.concatenate([table.reshape(lines * shards, -1) for table in second], axis=1)
    angle = d * b * (2.0 * math.pi / lags)
    fine = np.concatenate([np.cos(angle), np.sin(angle)], axis=1) * bins**-0.5
    high = fine.astype(jnp.bfloat16).astype(np.float64)
    fine = np.concatenate([high, fine - high])
    width = max(first.shape[1], second.shape[1], fine.shape[1])
    table = [np.pad(t, ((0, 0), (0, width - t.shape[1]))) for t in (first, second, fine)]
    return jnp.asarray(np.concatenate(table), jnp.bfloat16)


def body(spectra, pair_blocks, block_count):
    _, _, segments, parts, _, bins = spectra.shape
    slots = pair_blocks.shape[1]
    hours, stations = lax.axis_size("tm"), lax.axis_size("sta")
    near = 2
    shards = hours * near
    share = slots // hours
    run = bins // shards
    halves = run // LANES
    chunk_in = segments * halves * 2 * parts
    chunk_out = share * parts * parts * 2 * halves

    def shard(t, s):
        return t * near + s % near

    swap = [(s, s ^ 1) for s in range(stations)]
    pairs = pair_blocks[0].T
    other = lax.ppermute(pairs, "sta", swap)
    depth = stations * chunk_in

    owners = [shard(t, s) for t in range(hours) for s in range(stations)]
    white, mine, live = kernel_call(
        functools.partial(whiten_kernel, owners, shards, segments),
        (
            pltpu.VMEM((hours * stations, chunk_in, LANES), jnp.bfloat16),
            pltpu.VMEM((2, slots), jnp.int32),
            pltpu.VMEM((SLAB, LANES), jnp.int32),
        ),
        [HBM, HBM, pl.BlockSpec(memory_space=pltpu.SMEM)],
        [
            pltpu.VMEM((segments * parts, 2, bins), jnp.bfloat16),
            pltpu.VMEM((shards, chunk_in, LANES), jnp.float32),
            pltpu.SemaphoreType.DMA((2,)),
        ],
    )(in_hbm(spectra.reshape(segments * parts, 2, bins)), in_hbm(pairs), block_count)
    white, other = lax.optimization_barrier((white, other))
    every = lax.all_to_all(white, MESH_AXES, 0, 0, tiled=True)

    table = lag_table(bins, shards, share)
    daily, table = kernel_call(
        functools.partial(cross_kernel, segments, share),
        (
            pltpu.VMEM((shards, chunk_out, LANES), jnp.bfloat16),
            pltpu.VMEM(table.shape, table.dtype),
        ),
        [VMEM, VMEM, VMEM, HBM],
        [pltpu.VMEM((shards * chunk_out, LANES), jnp.float32), pltpu.SemaphoreType.DMA],
    )(mine, other, every.reshape(hours, depth, LANES), in_hbm(table))

    groups = [
        [t * stations + s + e for t in range(hours) for e in range(near)] for s in range(0, stations, near)
    ]
    whole = lax.all_to_all(daily, MESH_AXES, 0, 0, tiled=True, axis_index_groups=groups)

    result = kernel_call(
        lag_kernel,
        jax.ShapeDtypeStruct((parts, parts, share, 2 * bins), jnp.bfloat16),
        [VMEM] * 3,
        [pltpu.VMEM((shards * chunk_out, LANES), jnp.float32)],
    )(live, whole.reshape(shards * chunk_out, LANES), table)
    return result.transpose(2, 0, 1, 3).reshape(1, share, 1, 1, parts, parts, 2 * bins)


def solution(mesh):
    placed = (P("tm", "sta", None, None, None, None), P("sta", None, None), P("sta"))
    return jax.shard_map(
        body,
        mesh=mesh,
        in_specs=placed,
        out_specs=P("sta", "tm", None, None, None, None, None),
        check_vma=False,
    )
```

time: 32.1 us -> 29 us (0.903)
  blocking collectives: 0 us -> 23.7 us
  waiting for transfers between devices: 13 us -> 0.01 us
  starting transfers between devices: 11 us -> 0.45 us
  local copies, waits for them, and re-layouts: 3.39 us -> 0 us
  Pallas kernels: 3.62 us -> 3.95 us
    all_to_all x0 -> x2, blocking collectives: none -> 23.7 us  [the longest x1 15.5 us: body(): every = lax.all_to_all(white, MESH_AXES, 0, 0, tiled=True)]
    all_to_all x2 -> x0, waiting for transfers between devices: 12.2 us -> none  [the longest x1 7.22 us: body(): every = lax.all_to_all(white, MESH_AXES, 0, 0, tiled=True)]
    all_to_all x2 -> x0, starting transfers between devices: 10.7 us -> none  [the longest x1 7.3 us: body(): every = lax.all_to_all(white, MESH_AXES, 0, 0, tiled=True)]
    another operation x1 -> x0, local copies, waits for them, and re-layouts: 1.71 us -> none  [body(): spectra[0, 0].reshape(segments, parts, 2, run, shards)]
    reshape x2 -> x0, local copies, waits for them, and re-layouts: 0.9 us -> none  [the longest x1 0.85 us: body(): return result.reshape(1, share, 1, 1, parts, parts, 2 * bins)]
    ppermute x1, waiting for transfers between devices: 0.81 us -> 0.01 us  [body(): other = lax.ppermute(pairs, 'sta', swap)]
    pallas_call x3, Pallas kernels: 3.62 us -> 3.95 us  [the longest x1 1.37 us: body(): kernel_call(functools.partial(whiten_kernel, owners, shards, segments), (...]
  transfers between devices with their start and end apart: 3 -> 1, of which waited for: 3 -> 0; matrix products, arithmetic and copies ran while one was open for 1% -> 0% of each run, Pallas kernels for 0% -> 5%
where the time goes in v2:
time: 29 us; the launch traced here: 28.8 us
  blocking collectives  23.7 us (82%)
  Pallas kernels  3.95 us (14%)
  between operations  0.68 us (2%)
  starting transfers between devices  0.45 us (2%)
    all_to_all x1, blocking collectives, body(): every = lax.all_to_all(white, MESH_AXES, 0, 0, tiled=True)  15.5 us
    all_to_all x1, blocking collectives, body(): lax.all_to_all(daily, MESH_AXES, 0, 0, tiled=True, axis_index_groups=groups)  8.19 us
    pallas_call x1, Pallas kernels, body(): kernel_call(functools.partial(whiten_kernel, owners, shards, segments), (...  1.37 us
    pallas_call x1, Pallas kernels, body(): kernel_call(functools.partial(cross_kernel, segments, share), (pltpu.VMEM...  1.35 us
    pallas_call x1, Pallas kernels, body(): kernel_call(lag_kernel, jax.ShapeDtypeStruct((parts, parts, share, 2 * bi...  1.24 us
  transfers between devices with their start and end apart: 1, of which 0 were waited for; matrix products, arithmetic and copies ran while one was open for 0% of the time, Pallas kernels for 5%

profile of v2, /device:TPU:0, one launch (start us, length us, event | category | flops | bytes accessed | tf_op | source)
XLA Modules:
  0.0 28.8 jit_solution(2344584779226042443)
XLA Ops:
  0.0 0.5 %collective-permute-start = (s32[2,8]{1,0:T(2,128)}, s32[2,8]{1,0:T(2,128)S(1)}, u32[]{:S(2)}, u32[]{:S(2)}) collective-permute-start(s32[2,8]{1,0:T(2,128)} %bitcast.12), channel_id=1, source_target_pairs={{0,1},{1,0},{2,3},{3,2},{4,5},{5,4},{6,7},{7,6},{8,9},{9,8},{10,11... | collective-permute-start | bytes 200 | tf_op jit(solution)/shard_map/ppermute | solution.py:247
  1.1 1.4 %shard_map.46 = (bf16[32,24,128]{2,1,0:T(8,128)(2,1)S(1)}, s32[2,8]{1,0:T(2,128)S(1)}, s32[8,128]{1,0:T(8,128)S(1)}) custom-call(bf16[6,2,2048]{2,1,0:T(2,128)(2,1)} %bitcast.11, s32[2,8]{1,0:T(2,128)} %bitcast.13, s32[1]{0:T(128)S(6)} %copy.5.count_ref), custom_call_target="tpu_custom_call" | custom-call | tf_op jit(solution)/shard_map/pallas_call | solution.py:251
  2.5 0.0 collective-permute-done.other_ref
  2.5 15.5 %all_to_all.10 = bf16[32,24,128]{2,1,0:T(8,128)(2,1)S(1)} all-to-all(bf16[32,24,128]{2,1,0:T(8,128)(2,1)S(1)} %get-tuple-element.16), channel_id=1, replica_groups=mesh['tm'=4,'sta'=8] {'tm','sta'}, dimensions={0} | all-to-all | bytes 393216 | tf_op jit(solution)/shard_map/all_to_all | solution.py:266
  18.0 1.3 %shard_map.47 = (bf16[8,72,128]{2,1,0:T(8,128)(2,1)S(1)}, bf16[672,1024]{1,0:T(8,128)(2,1)S(1)}) custom-call(s32[2,8]{1,0:T(2,128)S(1)} %get-tuple-element.13.mine_ref, s32[2,8]{1,0:T(2,128)S(1)} %collective-permute-done.other_ref, bf16[4,192,128]{2,1,0:T(8,128)(2,1)S(1)} %bitcast.9, bf16[672,1024]{1,0:T(8,128)(2,1)} %constant.2.clone.table_ref), custom_call_target="tpu_custom_call" | custom-call | tf_op jit(solution)/shard_map/pallas_call | solution.py:269
  19.4 8.2 %all_to_all.11 = bf16[8,72,128]{2,1,0:T(8,128)(2,1)S(1)} all-to-all(bf16[8,72,128]{2,1,0:T(8,128)(2,1)S(1)} %get-tuple-element.17), channel_id=1, replica_groups={{0,1,8,9,16,17,24,25},{2,3,10,11,18,19,26,27},{4,5,12,13,20,21,28,29},{..., dimensions={0} | all-to-all | bytes 294912 | tf_op jit(solution)/shard_map/all_to_all | solution.py:282
  27.6 1.2 %shard_map.48 = bf16[3,3,2,4096]{3,2,1,0:T(2,128)(2,1)} custom-call(s32[8,128]{1,0:T(8,128)S(1)} %get-tuple-element.12.live_ref, bf16[576,128]{1,0:T(8,128)(2,1)S(1)} %bitcast.10, bf16[672,1024]{1,0:T(8,128)(2,1)S(1)} %get-tuple-element.18.table_ref), custom_call_target="tpu_custom_call" | custom-call | tf_op jit(solution)/shard_map/pallas_call | solution.py:284
Async XLA Ops:
  0.0 2.5 %collective-permute-start = (s32[2,8]{1,0:T(2,128)}, s32[2,8]{1,0:T(2,128)S(1)}, u32[]{:S(2)}, u32[]{:S(2)}) collective-permute-start(s32[2,8]{1,0:T(2,128)} %bitcast.12), channel_id=1, source_target_pairs={{0,1},{1,0},{2,3},{3,2},{4,5},{5,4},{6,7},{7,6},{8,9},{9,8},{10,11... | collective-permute-start | bytes 200 | tf_op jit(solution)/shard_map/ppermute | solution.py:247

commit v3 on v2

--- a/solution.py
+++ b/solution.py
@@ -24,26 +24,26 @@
     return pltpu.with_memory_space_constraint(array, pltpu.HBM)
 
 
-def kernel_call(kernel, out_shape, in_specs, scratch):
+def kernel_call(kernel, out_shape, in_specs, scratch, out_spec=VMEM):
     return pl.pallas_call(
         kernel,
         out_shape=out_shape,
         in_specs=in_specs,
-        out_specs=jax.tree.map(lambda _: VMEM, out_shape),
+        out_specs=jax.tree.map(lambda _: out_spec, out_shape),
         scratch_shapes=scratch,
         compiler_params=pltpu.CompilerParams(vmem_limit_bytes=40 * 1024 * 1024),
     )
 
 
 def whiten_kernel(
-    owners, shards, segments, spectra_ref, pairs_ref, count_ref, o_ref, mine_ref, live_ref, x_ref, rows, sems
+    owners, shards, segments, spectra_ref, pairs_ref, count_ref, *refs
 ):
+    first_ref, second_ref, o_ref, mine_ref, live_ref, first_held, second_held, x_ref, rows, sems = refs
     bins = x_ref.shape[2]
     tiles = bins // LANES
-    copies = [
-        pltpu.make_async_copy(source, target, sems.at[n])
-        for n, (source, target) in enumerate(((spectra_ref, x_ref), (pairs_ref, mine_ref)))
-    ]
+    moves = [(spectra_ref.at[pl.ds(g * PARTS, PARTS)], x_ref.at[pl.ds(g * PARTS, PARTS)]) for g in range(segments)]
+    moves += [(pairs_ref, mine_ref), (first_ref, first_held), (second_ref, second_held)]
+    copies = [pltpu.make_async_copy(*move, sems.at[n]) for n, move in enumerate(moves)]
     for copy in copies:
         copy.start()
     lane = lax.broadcasted_iota(jnp.int32, (SLAB, LANES), 1)
@@ -53,9 +53,9 @@
     apart = lax.broadcasted_iota(jnp.int32, (3 * LANES, LANES), 0) - LANES
     apart = apart - lax.broadcasted_iota(jnp.int32, (3 * LANES, LANES), 1)
     band = (jnp.abs(apart) <= SMOOTH).astype(jnp.bfloat16)
-    copies[0].wait()
     values, blocks = [], []
     for g in range(segments):
+        copies[g].wait()
         lines = [x_ref[g * PARTS + x].astype(jnp.float32) for x in range(PARTS)]
         lines = jnp.concatenate(lines + [jnp.zeros((SLAB - 2 * PARTS, bins), jnp.float32)], axis=0)
         value = [lines[:, v * LANES : (v + 1) * LANES] for v in range(tiles)]
@@ -96,7 +96,8 @@
     packed = rows[...].astype(jnp.bfloat16)
     for device, d in enumerate(owners):
         o_ref[device] = packed[d]
-    copies[1].wait()
+    for copy in copies[segments:]:
+        copy.wait()
     live_ref[...] = jnp.full(live_ref.shape, count_ref[0])
 
 
@@ -117,10 +118,8 @@
     return columns
 
 
-def cross_kernel(segments, share, mine_ref, other_ref, w_ref, table_ref, o_ref, held_ref, rows, sem):
+def cross_kernel(segments, share, mine_ref, other_ref, w_ref, o_ref, rows):
     hours, depth, _ = w_ref.shape
-    table_copy = pltpu.make_async_copy(table_ref, held_ref, sem)
-    table_copy.start()
     group, chunk, _ = o_ref.shape
     slots = group * share
     kinds = 2 * PARTS
@@ -132,9 +131,11 @@
         offset = column - station * blocks
         sides.append([(offset == r).astype(jnp.bfloat16) for r in range(blocks)])
     chosen = jnp.concatenate(sides[0] + sides[1], axis=0)
-    picked = [
-        jnp.dot(chosen, w_ref[h], preferred_element_type=jnp.float32) for h in range(hours)
-    ]
+    picked = []
+    for h in range(0, hours, 2):
+        two = jnp.concatenate([w_ref[e] for e in range(h, min(h + 2, hours))], axis=1)
+        two = jnp.dot(chosen, two, preferred_element_type=jnp.float32)
+        picked += [two[:, e : e + LANES] for e in range(0, two.shape[1], LANES)]
 
     def part(side, h, g, j, c, x):
         first = (side * blocks + ((g * halves + j) * PARTS + x) * 2 + c) * slots
@@ -160,10 +161,9 @@
                     row = ((u * PARTS * PARTS + n) * 2 + c) * halves + j
                     rows[pl.ds(row, group, stride=chunk), :] = total[u * group : (u + 1) * group]
     o_ref[...] = rows[...].reshape(o_ref.shape).astype(jnp.bfloat16)
-    table_copy.wait()
-
-
-def lag_kernel(live_ref, d_ref, table_ref, o_ref, rows):
+
+
+def lag_kernel(live_ref, d_ref, first_ref, second_ref, o_ref, rows, lags_ref, sems):
     share, lags = o_ref.shape[2:]
     shards = lax.axis_size("tm") * 2
     period = lags // shards
@@ -175,11 +175,13 @@
     for k in range(pieces):
         column = [rows[pl.ds(r * pieces + k, shards, stride=lines * pieces), :] for r in range(lines)]
         daily.append(jnp.concatenate(column, axis=0).astype(jnp.bfloat16))
-    daily = jnp.concatenate(daily, axis=1)
-    middle = jnp.dot(daily, table_ref[:period, : 2 * period], preferred_element_type=jnp.float32)
-    middle = middle.reshape(lines, shards, 2 * period)
-    re, im = middle[:, :, :period], middle[:, :, period:]
-    turn = table_ref[period + total : period + total + 2 * shards, : 2 * period].astype(jnp.float32)
+    half = pieces // 2
+    daily = jnp.concatenate([jnp.concatenate(daily[c * half : (c + 1) * half], axis=1) for c in range(2)], axis=0)
+    run = period // 2
+    middle = jnp.dot(daily, first_ref[:run], preferred_element_type=jnp.float32)
+    re = (middle[:total, :period] - middle[total:, period:]).reshape(lines, shards, period)
+    im = (middle[:total, period:] + middle[total:, :period]).reshape(lines, shards, period)
+    turn = first_ref[run : run + 2 * shards].astype(jnp.float32)
     turn = turn[:shards] + turn[shards:]
     cos, sin = turn[None, :, :period], turn[None, :, period:]
     turned = jnp.concatenate(
@@ -189,19 +191,28 @@
         ],
         axis=0,
     )
-    second = table_ref[period : period + total, : 2 * total]
-    joined = jnp.dot(second, turned, preferred_element_type=jnp.float32)
     live = live_ref[:1, :1] - lax.axis_index("tm") * share
-    slot = lax.broadcasted_iota(jnp.int32, joined.shape, 0) % share
-    joined = jnp.where(slot < live, joined, 0.0)
-    for a in range(shards):
-        for n in range(PARTS * PARTS):
-            first = (a * PARTS * PARTS + n) * share
-            value = joined[first : first + share].astype(jnp.bfloat16)
-            o_ref[n // PARTS, n % PARTS, :, a * period : (a + 1) * period] = value
-
-
-def lag_table(bins, shards, share):
+    cuts = sems.shape[0]
+    depth = total // cuts
+    slot = lax.broadcasted_iota(jnp.int32, (depth, period), 0) % share
+    copies = []
+    for cut in range(cuts):
+        joined = jnp.dot(second_ref[cut * depth : (cut + 1) * depth], turned, preferred_element_type=jnp.float32)
+        joined = jnp.where(slot < live, joined, 0.0)
+        base = cut * (lags // cuts)
+        for a in range(shards // cuts):
+            for n in range(PARTS * PARTS):
+                first = (a * PARTS * PARTS + n) * share
+                value = joined[first : first + share].astype(jnp.bfloat16)
+                lags_ref[n // PARTS, n % PARTS, :, base + a * period : base + (a + 1) * period] = value
+        window = (slice(None),) * 3 + (pl.ds(base, lags // cuts),)
+        copies.append(pltpu.make_async_copy(lags_ref.at[window], o_ref.at[window], sems.at[cut]))
+        copies[-1].start()
+    for copy in copies:
+        copy.wait()
+
+
+def lag_tables(bins, shards, share):
     lags = 2 * bins
     period = lags // shards
     lines = share * PARTS * PARTS
@@ -209,22 +220,20 @@
     inner = lane % shards * (LANES // shards) + lane // shards
     k = (np.arange(0, bins // shards, LANES)[:, None] + inner).reshape(-1, 1)
     b = np.arange(period)[None, :]
-    angle = (k * b % period) * (2.0 * math.pi / period)
-    cos, sin = np.cos(angle), np.sin(angle)
-    first = np.block([[cos, sin], [-sin, cos]])
     d = np.arange(shards)[:, None]
+
+    def turns(angle):
+        return np.concatenate([np.cos(angle), np.sin(angle)], axis=1)
+
+    fine = turns(d * b * (2.0 * math.pi / lags)) * bins**-0.5
+    high = fine.astype(jnp.bfloat16).astype(np.float64)
+    first = np.concatenate([turns((k * b % period) * (2.0 * math.pi / period)), high, fine - high])
     a = np.arange(shards)[:, None] - bins // period
     turn = (a * d.T % shards) * (2.0 * math.pi / shards)
     same = np.eye(lines).reshape(share, PARTS * PARTS, lines).transpose(1, 0, 2)
     second = [np.einsum("ad,nur->anurd", table, same) for table in (np.cos(turn), -np.sin(turn))]
     second = np.concatenate([table.reshape(lines * shards, -1) for table in second], axis=1)
-    angle = d * b * (2.0 * math.pi / lags)
-    fine = np.concatenate([np.cos(angle), np.sin(angle)], axis=1) * bins**-0.5
-    high = fine.astype(jnp.bfloat16).astype(np.float64)
-    fine = np.concatenate([high, fine - high])
-    width = max(first.shape[1], second.shape[1], fine.shape[1])
-    table = [np.pad(t, ((0, 0), (0, width - t.shape[1]))) for t in (first, second, fine)]
-    return jnp.asarray(np.concatenate(table), jnp.bfloat16)
+    return jnp.asarray(first, jnp.bfloat16), jnp.asarray(second, jnp.bfloat16)
 
 
 def body(spectra, pair_blocks, block_count):
@@ -244,37 +253,42 @@
 
     swap = [(s, s ^ 1) for s in range(stations)]
     pairs = pair_blocks[0].T
-    other = lax.ppermute(pairs, "sta", swap)
+    other = lax.ppermute(pair_blocks, "sta", swap)[0].T
     depth = stations * chunk_in
 
     owners = [shard(t, s) for t in range(hours) for s in range(stations)]
-    white, mine, live = kernel_call(
+    first, second = lag_tables(bins, shards, share)
+    white, mine, live, first, second = kernel_call(
         functools.partial(whiten_kernel, owners, shards, segments),
         (
             pltpu.VMEM((hours * stations, chunk_in, LANES), jnp.bfloat16),
             pltpu.VMEM((2, slots), jnp.int32),
             pltpu.VMEM((SLAB, LANES), jnp.int32),
+            pltpu.VMEM(first.shape, first.dtype),
+            pltpu.VMEM(second.shape, second.dtype),
         ),
-        [HBM, HBM, pl.BlockSpec(memory_space=pltpu.SMEM)],
+        [HBM, HBM, pl.BlockSpec(memory_space=pltpu.SMEM), HBM, HBM],
         [
             pltpu.VMEM((segments * parts, 2, bins), jnp.bfloat16),
             pltpu.VMEM((shards, chunk_in, LANES), jnp.float32),
-            pltpu.SemaphoreType.DMA((2,)),
+            pltpu.SemaphoreType.DMA((segments + 3,)),
         ],
-    )(in_hbm(spectra.reshape(segments * parts, 2, bins)), in_hbm(pairs), block_count)
+    )(
+        in_hbm(spectra.reshape(segments * parts, 2, bins)),
+        in_hbm(pairs),
+        block_count,
+        in_hbm(first),
+        in_hbm(second),
+    )
     white, other = lax.optimization_barrier((white, other))
     every = lax.all_to_all(white, MESH_AXES, 0, 0, tiled=True)
 
-    table = lag_table(bins, shards, share)
-    daily, table = kernel_call(
+    daily = kernel_call(
         functools.partial(cross_kernel, segments, share),
-        (
-            pltpu.VMEM((shards, chunk_out, LANES), jnp.bfloat16),
-            pltpu.VMEM(table.shape, table.dtype),
-        ),
-        [VMEM, VMEM, VMEM, HBM],
-        [pltpu.VMEM((shards * chunk_out, LANES), jnp.float32), pltpu.SemaphoreType.DMA],
-    )(mine, other, every.reshape(hours, depth, LANES), in_hbm(table))
+        pltpu.VMEM((shards, chunk_out, LANES), jnp.bfloat16),
+        [VMEM] * 3,
+        [pltpu.VMEM((shards * chunk_out, LANES), jnp.float32)],
+    )(mine, other, every.reshape(hours, depth, LANES))
 
     groups = [
         [t * stations + s + e for t in range(hours) for e in range(near)] for s in range(0, stations, near)
@@ -284,9 +298,14 @@
     result = kernel_call(
         lag_kernel,
         jax.ShapeDtypeStruct((parts, parts, share, 2 * bins), jnp.bfloat16),
-        [VMEM] * 3,
-        [pltpu.VMEM((shards * chunk_out, LANES), jnp.float32)],
-    )(live, whole.reshape(shards * chunk_out, LANES), table)
+        [VMEM] * 4,
+        [
+            pltpu.VMEM((shards * chunk_out, LANES), jnp.float32),
+            pltpu.VMEM((parts, parts, share, 2 * bins), jnp.bfloat16),
+            pltpu.SemaphoreType.DMA((2,)),
+        ],
+        pl.BlockSpec(memory_space=pl.ANY),
+    )(live, whole.reshape(shards * chunk_out, LANES), first, second)
     return result.transpose(2, 0, 1, 3).reshape(1, share, 1, 1, parts, parts, 2 * bins)
 
 

time: 29 us -> 28.4 us (0.979)
  Pallas kernels: 3.95 us -> 3.38 us
    pallas_call x1, Pallas kernels: 1.35 us -> 0.78 us  [body(): kernel_call(functools.partial(cross_kernel, segments, share), pltpu.VMEM(...]
where the time goes in v3:
time: 28.4 us; the launch traced here: 28.2 us
  blocking collectives  23.7 us (83%)
  Pallas kernels  3.38 us (12%)
  between operations  0.68 us (2%)
  starting transfers between devices  0.45 us (2%)
    all_to_all x1, blocking collectives, body(): every = lax.all_to_all(white, MESH_AXES, 0, 0, tiled=True)  15.5 us
    all_to_all x1, blocking collectives, body(): lax.all_to_all(daily, MESH_AXES, 0, 0, tiled=True, axis_index_groups=groups)  8.19 us
    pallas_call x1, Pallas kernels, body(): kernel_call(functools.partial(whiten_kernel, owners, shards, segments), (...  1.34 us
    pallas_call x1, Pallas kernels, body(): kernel_call(lag_kernel, jax.ShapeDtypeStruct((parts, parts, share, 2 * bi...  1.26 us
    pallas_call x1, Pallas kernels, body(): kernel_call(functools.partial(cross_kernel, segments, share), pltpu.VMEM(...  0.78 us
  transfers between devices with their start and end apart: 1, of which 0 were waited for; matrix products, arithmetic and copies ran while one was open for 0% of the time, Pallas kernels for 5%

profile of v3, /device:TPU:0, one launch (start us, length us, event | category | flops | bytes accessed | tf_op | source)
XLA Modules:
  0.0 28.2 jit_solution(9924072126905948816)
XLA Ops:
  0.0 0.5 %collective-permute-start = (s32[1,8,2]{1,2,0:T(2,128)}, s32[1,8,2]{1,2,0:T(2,128)S(1)}, u32[]{:S(2)}, u32[]{:S(2)}) collective-permute-start(s32[1,8,2]{1,2,0:T(2,128)} %param.6), channel_id=1, source_target_pairs={{0,1},{1,0},{2,3},{3,2},{4,5},{5,4},{6,7},{7,6},{8,9},{9,8},{10,11... | collective-permute-start | bytes 200 | tf_op jit(solution)/shard_map/ppermute | solution.py:256
  1.1 1.3 %shard_map.55 = (bf16[32,24,128]{2,1,0:T(8,128)(2,1)S(1)}, s32[2,8]{1,0:T(2,128)S(1)}, s32[8,128]{1,0:T(8,128)S(1)}, bf16[272,1024]{1,0:T(8,128)(2,1)S(1)}, bf16[144,288]{1,0:T(8,128)(2,1)S(1)}) custom-call(bf16[6,2,2048]{2,1,0:T(2,128)(2,1)} %bitcast.15, s32[2,8]{1,0:T(2,128)} %bitcast.16, s32[1]{0:T(128)S(6)} %copy.6.count_ref, ...), custom_call_target="tpu_custom_call" | custom-call | tf_op jit(solution)/shard_map/pallas_call | solution.py:261
  2.5 0.0 collective-permute-done
  2.5 15.5 %all_to_all.10 = bf16[32,24,128]{2,1,0:T(8,128)(2,1)S(1)} all-to-all(bf16[32,24,128]{2,1,0:T(8,128)(2,1)S(1)} %get-tuple-element.16), channel_id=1, replica_groups=mesh['tm'=4,'sta'=8] {'tm','sta'}, dimensions={0} | all-to-all | bytes 393216 | tf_op jit(solution)/shard_map/all_to_all | solution.py:284
  18.0 0.8 %shard_map.56 = bf16[8,72,128]{2,1,0:T(8,128)(2,1)S(1)} custom-call(s32[2,8]{1,0:T(2,128)S(1)} %get-tuple-element.13.mine_ref, s32[2,8]{1,0:T(2,128)S(1)} %bitcast.14, bf16[4,192,128]{2,1,0:T(8,128)(2,1)S(1)} %bitcast.12), custom_call_target="tpu_custom_call" | custom-call | tf_op jit(solution)/shard_map/pallas_call | solution.py:286
  18.8 8.2 %all_to_all.11 = bf16[8,72,128]{2,1,0:T(8,128)(2,1)S(1)} all-to-all(bf16[8,72,128]{2,1,0:T(8,128)(2,1)S(1)} %shard_map.56), channel_id=1, replica_groups={{0,1,8,9,16,17,24,25},{2,3,10,11,18,19,26,27},{4,5,12,13,20,21,28,29},{..., dimensions={0} | all-to-all | bytes 294912 | tf_op jit(solution)/shard_map/all_to_all | solution.py:296
  27.0 1.3 %shard_map.57 = bf16[3,3,2,4096]{3,2,1,0:T(2,128)(2,1)} custom-call(s32[8,128]{1,0:T(8,128)S(1)} %get-tuple-element.12.live_ref, bf16[576,128]{1,0:T(8,128)(2,1)S(1)} %bitcast.13, bf16[272,1024]{1,0:T(8,128)(2,1)S(1)} %get-tuple-element.17.first_ref, bf16[144,288]{1,0:T(8,128)(2,1)S(1)} %get-tuple-element.18.second_ref), custom_call_target="tpu_custom_call" | custom-call | tf_op jit(solution)/shard_map/pallas_call | solution.py:298
Async XLA Ops:
  0.0 2.5 %collective-permute-start = (s32[1,8,2]{1,2,0:T(2,128)}, s32[1,8,2]{1,2,0:T(2,128)S(1)}, u32[]{:S(2)}, u32[]{:S(2)}) collective-permute-start(s32[1,8,2]{1,2,0:T(2,128)} %param.6), channel_id=1, source_target_pairs={{0,1},{1,0},{2,3},{3,2},{4,5},{5,4},{6,7},{7,6},{8,9},{9,8},{10,11... | collective-permute-start | bytes 200 | tf_op jit(solution)/shard_map/ppermute | solution.py:256

commit v4 on v3

--- a/solution.py
+++ b/solution.py
@@ -106,8 +106,9 @@
     rows = share * hours * near
     lane = lax.broadcasted_iota(jnp.int32, (rows, hours * share), 1)
     row = lax.broadcasted_iota(jnp.int32, (rows, hours * share), 0)
-    owner = row % near
-    slot = row // near % hours * share + row // (near * hours)
+    place = hours * near - 1 - row % (hours * near)
+    owner = place % near
+    slot = place // near * share + row // (near * hours)
     second = lax.axis_index("sta") % near == 1
     columns = []
     for side in range(2):
@@ -119,21 +120,23 @@
 
 
 def cross_kernel(segments, share, mine_ref, other_ref, w_ref, o_ref, rows):
-    hours, depth, _ = w_ref.shape
+    early, stations, late, blocks, _ = w_ref.shape
+    hours, depth = early * late, stations * blocks
+    near = 2
     group, chunk, _ = o_ref.shape
     slots = group * share
-    kinds = 2 * PARTS
     halves = chunk // (share * PARTS * PARTS * 2)
-    blocks = segments * halves * kinds
     column = lax.broadcasted_iota(jnp.int32, (slots, depth), 1)
     sides = []
     for station in station_columns((mine_ref, other_ref), hours, share):
-        offset = column - station * blocks
+        place = station % near * (stations // near) + station // near
+        offset = column - place * blocks
         sides.append([(offset == r).astype(jnp.bfloat16) for r in range(blocks)])
     chosen = jnp.concatenate(sides[0] + sides[1], axis=0)
     picked = []
     for h in range(0, hours, 2):
-        two = jnp.concatenate([w_ref[e] for e in range(h, min(h + 2, hours))], axis=1)
+        two = [w_ref[e // late, :, e % late].reshape(depth, LANES) for e in range(h, min(h + 2, hours))]
+        two = jnp.concatenate(two, axis=1)
         two = jnp.dot(chosen, two, preferred_element_type=jnp.float32)
         picked += [two[:, e : e + LANES] for e in range(0, two.shape[1], LANES)]
 
@@ -248,15 +251,24 @@
     chunk_in = segments * halves * 2 * parts
     chunk_out = share * parts * parts * 2 * halves
 
+    early = 2 if hours % 2 == 0 else 1
+    late = hours // early
+    order = [
+        (th * late + tl, z * near + core)
+        for th in range(early)
+        for core in range(near)
+        for z in range(stations // near)
+        for tl in range(late)
+    ]
+
     def shard(t, s):
-        return t * near + s % near
+        return shards - 1 - (t * near + s % near)
 
     swap = [(s, s ^ 1) for s in range(stations)]
     pairs = pair_blocks[0].T
     other = lax.ppermute(pair_blocks, "sta", swap)[0].T
-    depth = stations * chunk_in
-
-    owners = [shard(t, s) for t in range(hours) for s in range(stations)]
+
+    owners = [shard(t, s) for t, s in order]
     first, second = lag_tables(bins, shards, share)
     white, mine, live, first, second = kernel_call(
         functools.partial(whiten_kernel, owners, shards, segments),
@@ -281,17 +293,19 @@
         in_hbm(second),
     )
     white, other = lax.optimization_barrier((white, other))
-    every = lax.all_to_all(white, MESH_AXES, 0, 0, tiled=True)
+    groups = [[t * stations + s for t, s in order]]
+    every = lax.all_to_all(white, MESH_AXES, 0, 0, tiled=True, axis_index_groups=groups)
 
     daily = kernel_call(
         functools.partial(cross_kernel, segments, share),
         pltpu.VMEM((shards, chunk_out, LANES), jnp.bfloat16),
         [VMEM] * 3,
         [pltpu.VMEM((shards * chunk_out, LANES), jnp.float32)],
-    )(mine, other, every.reshape(hours, depth, LANES))
+    )(mine, other, every.reshape(early, stations, late, chunk_in, LANES))
 
     groups = [
-        [t * stations + s + e for t in range(hours) for e in range(near)] for s in range(0, stations, near)
+        [t * stations + s + e for t in reversed(range(hours)) for e in reversed(range(near))]
+        for s in range(0, stations, near)
     ]
     whole = lax.all_to_all(daily, MESH_AXES, 0, 0, tiled=True, axis_index_groups=groups)
 

time: 28.4 us -> 27.2 us (0.958)
  blocking collectives: 23.7 us -> 22.4 us
    all_to_all x1, blocking collectives: 8.19 us -> 7.11 us  [body(): lax.all_to_all(daily, MESH_AXES, 0, 0, tiled=True, axis_index_groups=groups)]
where the time goes in v4:
time: 27.2 us; the launch traced here: 27 us
  blocking collectives  22.4 us (82%)
  Pallas kernels  3.39 us (12%)
  between operations  0.68 us (2%)
  starting transfers between devices  0.45 us (2%)
    all_to_all x1, blocking collectives, body(): lax.all_to_all(white, MESH_AXES, 0, 0, tiled=True, axis_index_groups=groups)  15.3 us
    all_to_all x1, blocking collectives, body(): lax.all_to_all(daily, MESH_AXES, 0, 0, tiled=True, axis_index_groups=groups)  7.11 us
    pallas_call x1, Pallas kernels, body(): kernel_call(functools.partial(whiten_kernel, owners, shards, segments), (...  1.34 us
    pallas_call x1, Pallas kernels, body(): kernel_call(lag_kernel, jax.ShapeDtypeStruct((parts, parts, share, 2 * bi...  1.26 us
    pallas_call x1, Pallas kernels, body(): kernel_call(functools.partial(cross_kernel, segments, share), pltpu.VMEM(...  0.79 us
  transfers between devices with their start and end apart: 1, of which 0 were waited for; matrix products, arithmetic and copies ran while one was open for 0% of the time, Pallas kernels for 5%

profile of v4, /device:TPU:0, one launch (start us, length us, event | category | flops | bytes accessed | tf_op | source)
XLA Modules:
  0.0 27.0 jit_solution(13019144288903569102)
XLA Ops:
  0.0 0.5 %collective-permute-start = (s32[1,8,2]{1,2,0:T(2,128)}, s32[1,8,2]{1,2,0:T(2,128)S(1)}, u32[]{:S(2)}, u32[]{:S(2)}) collective-permute-start(s32[1,8,2]{1,2,0:T(2,128)} %param.6), channel_id=1, source_target_pairs={{0,1},{1,0},{2,3},{3,2},{4,5},{5,4},{6,7},{7,6},{8,9},{9,8},{10,11... | collective-permute-start | bytes 200 | tf_op jit(solution)/shard_map/ppermute | solution.py:269
  1.1 1.3 %shard_map.55 = (bf16[32,24,128]{2,1,0:T(8,128)(2,1)S(1)}, s32[2,8]{1,0:T(2,128)S(1)}, s32[8,128]{1,0:T(8,128)S(1)}, bf16[272,1024]{1,0:T(8,128)(2,1)S(1)}, bf16[144,288]{1,0:T(8,128)(2,1)S(1)}) custom-call(bf16[6,2,2048]{2,1,0:T(2,128)(2,1)} %bitcast.15, s32[2,8]{1,0:T(2,128)} %bitcast.16, s32[1]{0:T(128)S(6)} %copy.6.count_ref, ...), custom_call_target="tpu_custom_call" | custom-call | tf_op jit(solution)/shard_map/pallas_call | solution.py:273
  2.5 0.0 collective-permute-done
  2.5 15.3 %all_to_all.10 = bf16[32,24,128]{2,1,0:T(8,128)(2,1)S(1)} all-to-all(bf16[32,24,128]{2,1,0:T(8,128)(2,1)S(1)} %get-tuple-element.16), channel_id=1, replica_groups={{0,8,2,10,4,12,6,14,1,9,3,11,5,13,7,15,16,24,18,26,20,28,22,30,17,25,19..., dimensions={0} | all-to-all | bytes 393216 | tf_op jit(solution)/shard_map/all_to_all | solution.py:297
  17.8 0.8 %shard_map.56 = bf16[8,72,128]{2,1,0:T(8,128)(2,1)S(1)} custom-call(s32[2,8]{1,0:T(2,128)S(1)} %get-tuple-element.13.mine_ref, s32[2,8]{1,0:T(2,128)S(1)} %bitcast.14, bf16[2,8,2,24,128]{4,3,2,1,0:T(8,128)(2,1)S(1)} %bitcast.12), custom_call_target="tpu_custom_call" | custom-call | tf_op jit(solution)/shard_map/pallas_call | solution.py:299
  18.6 7.1 %all_to_all.11 = bf16[8,72,128]{2,1,0:T(8,128)(2,1)S(1)} all-to-all(bf16[8,72,128]{2,1,0:T(8,128)(2,1)S(1)} %shard_map.56), channel_id=1, replica_groups={{25,24,17,16,9,8,1,0},{27,26,19,18,11,10,3,2},{29,28,21,20,13,12,5,4},{..., dimensions={0} | all-to-all | bytes 294912 | tf_op jit(solution)/shard_map/all_to_all | solution.py:310
  25.7 1.3 %shard_map.57 = bf16[3,3,2,4096]{3,2,1,0:T(2,128)(2,1)} custom-call(s32[8,128]{1,0:T(8,128)S(1)} %get-tuple-element.12.live_ref, bf16[576,128]{1,0:T(8,128)(2,1)S(1)} %bitcast.13, bf16[272,1024]{1,0:T(8,128)(2,1)S(1)} %get-tuple-element.17.first_ref, bf16[144,288]{1,0:T(8,128)(2,1)S(1)} %get-tuple-element.18.second_ref), custom_call_target="tpu_custom_call" | custom-call | tf_op jit(solution)/shard_map/pallas_call | solution.py:312
Async XLA Ops:
  0.0 2.5 %collective-permute-start = (s32[1,8,2]{1,2,0:T(2,128)}, s32[1,8,2]{1,2,0:T(2,128)S(1)}, u32[]{:S(2)}, u32[]{:S(2)}) collective-permute-start(s32[1,8,2]{1,2,0:T(2,128)} %param.6), channel_id=1, source_target_pairs={{0,1},{1,0},{2,3},{3,2},{4,5},{5,4},{6,7},{7,6},{8,9},{9,8},{10,11... | collective-permute-start | bytes 200 | tf_op jit(solution)/shard_map/ppermute | solution.py:269

commit v5 on v4

--- a/solution.py
+++ b/solution.py
@@ -1,4 +1,5 @@
 import functools
+import itertools
 import math
 
 import jax
@@ -94,8 +95,10 @@
                     mixed = pltpu.roll(mixed, LANES - d, 1)
                 rows[d, first : first + 2 * PARTS] = mixed[: 2 * PARTS]
     packed = rows[...].astype(jnp.bfloat16)
-    for device, d in enumerate(owners):
-        o_ref[device] = packed[d]
+    lines = rows.shape[1]
+    for device, classes in enumerate(owners):
+        for e, d in enumerate(classes):
+            o_ref[device, e * lines : (e + 1) * lines] = packed[d]
     for copy in copies[segments:]:
         copy.wait()
     live_ref[...] = jnp.full(live_ref.shape, count_ref[0])
@@ -119,38 +122,43 @@
     return columns
 
 
+def station_place(station, stations, near):
+    chips = stations // near
+    return (near - 1 - station % near) * chips + (station // near + chips - chips // 2) % chips
+
+
 def cross_kernel(segments, share, mine_ref, other_ref, w_ref, o_ref, rows):
-    early, stations, late, blocks, _ = w_ref.shape
-    hours, depth = early * late, stations * blocks
+    hours, stations, classes, blocks, _ = w_ref.shape
+    depth = stations * blocks
     near = 2
     group, chunk, _ = o_ref.shape
     slots = group * share
-    halves = chunk // (share * PARTS * PARTS * 2)
+    halves = chunk // (classes * share * PARTS * PARTS * 2)
     column = lax.broadcasted_iota(jnp.int32, (slots, depth), 1)
     sides = []
-    for station in station_columns((mine_ref, other_ref), hours, share):
-        place = station % near * (stations // near) + station // near
+    for station in station_columns((mine_ref, other_ref), group // near, share):
+        place = station_place(station, stations, near)
         offset = column - place * blocks
         sides.append([(offset == r).astype(jnp.bfloat16) for r in range(blocks)])
     chosen = jnp.concatenate(sides[0] + sides[1], axis=0)
+    columns = [w_ref[h, :, e].reshape(depth, LANES) for h in range(hours) for e in range(classes)]
     picked = []
-    for h in range(0, hours, 2):
-        two = [w_ref[e // late, :, e % late].reshape(depth, LANES) for e in range(h, min(h + 2, hours))]
-        two = jnp.concatenate(two, axis=1)
+    for m in range(0, len(columns), 2):
+        two = jnp.concatenate(columns[m : m + 2], axis=1)
         two = jnp.dot(chosen, two, preferred_element_type=jnp.float32)
-        picked += [two[:, e : e + LANES] for e in range(0, two.shape[1], LANES)]
-
-    def part(side, h, g, j, c, x):
+        picked += [two[:, n : n + LANES] for n in range(0, two.shape[1], LANES)]
+
+    def part(side, h, e, g, j, c, x):
         first = (side * blocks + ((g * halves + j) * PARTS + x) * 2 + c) * slots
-        return picked[h][first : first + slots]
-
-    for j in range(halves):
+        return picked[h * classes + e][first : first + slots]
+
+    for e, j in itertools.product(range(classes), range(halves)):
         real = [None] * (PARTS * PARTS)
         imag = [None] * (PARTS * PARTS)
         for h in range(hours):
             for g in range(segments):
-                left = [[part(0, h, g, j, c, x) for x in range(PARTS)] for c in range(2)]
-                right = [[part(1, h, g, j, c, x) for x in range(PARTS)] for c in range(2)]
+                left = [[part(0, h, e, g, j, c, x) for x in range(PARTS)] for c in range(2)]
+                right = [[part(1, h, e, g, j, c, x) for x in range(PARTS)] for c in range(2)]
                 for x in range(PARTS):
                     for y in range(PARTS):
                         re = left[0][x] * right[0][y] + left[1][x] * right[1][y]
@@ -161,7 +169,7 @@
         for n in range(PARTS * PARTS):
             for c, total in enumerate((real[n], imag[n])):
                 for u in range(share):
-                    row = ((u * PARTS * PARTS + n) * 2 + c) * halves + j
+                    row = (((e * share + u) * PARTS * PARTS + n) * 2 + c) * halves + j
                     rows[pl.ds(row, group, stride=chunk), :] = total[u * group : (u + 1) * group]
     o_ref[...] = rows[...].reshape(o_ref.shape).astype(jnp.bfloat16)
 
@@ -171,9 +179,9 @@
     shards = lax.axis_size("tm") * 2
     period = lags // shards
     pieces = period // LANES
-    lines = d_ref.shape[0] // (pieces * shards)
+    lines = d_ref.shape[1] // (pieces * shards)
     total = lines * shards
-    rows[...] = d_ref[...].astype(jnp.float32)
+    rows[...] = sum(d_ref[h].astype(jnp.float32) for h in range(d_ref.shape[0]))
     daily = []
     for k in range(pieces):
         column = [rows[pl.ds(r * pieces + k, shards, stride=lines * pieces), :] for r in range(lines)]
@@ -253,27 +261,27 @@
 
     early = 2 if hours % 2 == 0 else 1
     late = hours // early
+    chips = stations // near
     order = [
-        (th * late + tl, z * near + core)
-        for th in range(early)
-        for core in range(near)
-        for z in range(stations // near)
-        for tl in range(late)
+        (t, (z + chips // 2) % chips * near + core)
+        for t in reversed(range(late))
+        for core in reversed(range(near))
+        for z in range(chips)
     ]
-
-    def shard(t, s):
-        return shards - 1 - (t * near + s % near)
 
     swap = [(s, s ^ 1) for s in range(stations)]
     pairs = pair_blocks[0].T
     other = lax.ppermute(pair_blocks, "sta", swap)[0].T
 
-    owners = [shard(t, s) for t, s in order]
+    pieces = late * near
+    owners = [
+        [(pieces - 1 - (t * near + s % near)) * early + e for e in range(early)] for t, s in order
+    ]
     first, second = lag_tables(bins, shards, share)
     white, mine, live, first, second = kernel_call(
         functools.partial(whiten_kernel, owners, shards, segments),
         (
-            pltpu.VMEM((hours * stations, chunk_in, LANES), jnp.bfloat16),
+            pltpu.VMEM((late * stations, early * chunk_in, LANES), jnp.bfloat16),
             pltpu.VMEM((2, slots), jnp.int32),
             pltpu.VMEM((SLAB, LANES), jnp.int32),
             pltpu.VMEM(first.shape, first.dtype),
@@ -293,15 +301,15 @@
         in_hbm(second),
     )
     white, other = lax.optimization_barrier((white, other))
-    groups = [[t * stations + s for t, s in order]]
+    groups = [[(h * late + t) * stations + s for t, s in order] for h in range(early)]
     every = lax.all_to_all(white, MESH_AXES, 0, 0, tiled=True, axis_index_groups=groups)
 
     daily = kernel_call(
         functools.partial(cross_kernel, segments, share),
-        pltpu.VMEM((shards, chunk_out, LANES), jnp.bfloat16),
+        pltpu.VMEM((shards, early * chunk_out, LANES), jnp.bfloat16),
         [VMEM] * 3,
-        [pltpu.VMEM((shards * chunk_out, LANES), jnp.float32)],
-    )(mine, other, every.reshape(early, stations, late, chunk_in, LANES))
+        [pltpu.VMEM((shards * early * chunk_out, LANES), jnp.float32)],
+    )(mine, other, every.reshape(late, stations, early, chunk_in, LANES))
 
     groups = [
         [t * stations + s + e for t in reversed(range(hours)) for e in reversed(range(near))]
@@ -319,7 +327,7 @@
             pltpu.SemaphoreType.DMA((2,)),
         ],
         pl.BlockSpec(memory_space=pl.ANY),
-    )(live, whole.reshape(shards * chunk_out, LANES), first, second)
+    )(live, whole.reshape(early, shards * chunk_out, LANES), first, second)
     return result.transpose(2, 0, 1, 3).reshape(1, share, 1, 1, parts, parts, 2 * bins)
 
 

time: 27.2 us -> 26.5 us (0.974)
  blocking collectives: 22.4 us -> 21.6 us
    all_to_all x1, blocking collectives: 15.3 us -> 13 us  [body(): lax.all_to_all(white, MESH_AXES, 0, 0, tiled=True, axis_index_groups=groups)]
    all_to_all x1, blocking collectives: 7.11 us -> 8.57 us  [body(): lax.all_to_all(daily, MESH_AXES, 0, 0, tiled=True, axis_index_groups=groups)]
where the time goes in v5:
time: 26.5 us; the launch traced here: 26.3 us
  blocking collectives  21.6 us (82%)
  Pallas kernels  3.52 us (13%)
  between operations  0.68 us (3%)
  starting transfers between devices  0.45 us (2%)
    all_to_all x1, blocking collectives, body(): lax.all_to_all(white, MESH_AXES, 0, 0, tiled=True, axis_index_groups=groups)  13 us
    all_to_all x1, blocking collectives, body(): lax.all_to_all(daily, MESH_AXES, 0, 0, tiled=True, axis_index_groups=groups)  8.57 us
    pallas_call x1, Pallas kernels, body(): kernel_call(functools.partial(whiten_kernel, owners, shards, segments), (...  1.34 us
    pallas_call x1, Pallas kernels, body(): kernel_call(lag_kernel, jax.ShapeDtypeStruct((parts, parts, share, 2 * bi...  1.26 us
    pallas_call x1, Pallas kernels, body(): kernel_call(functools.partial(cross_kernel, segments, share), pltpu.VMEM(...  0.91 us
  transfers between devices with their start and end apart: 1, of which 0 were waited for; matrix products, arithmetic and copies ran while one was open for 0% of the time, Pallas kernels for 5%

profile of v5, /device:TPU:0, one launch (start us, length us, event | category | flops | bytes accessed | tf_op | source)
XLA Modules:
  0.0 26.3 jit_solution(3870817989978501706)
XLA Ops:
  0.0 0.5 %collective-permute-start = (s32[1,8,2]{1,2,0:T(2,128)}, s32[1,8,2]{1,2,0:T(2,128)S(1)}, u32[]{:S(2)}, u32[]{:S(2)}) collective-permute-start(s32[1,8,2]{1,2,0:T(2,128)} %param.6), channel_id=1, source_target_pairs={{0,1},{1,0},{2,3},{3,2},{4,5},{5,4},{6,7},{7,6},{8,9},{9,8},{10,11... | collective-permute-start | bytes 200 | tf_op jit(solution)/shard_map/ppermute | solution.py:274
  1.1 1.3 %shard_map.55 = (bf16[16,48,128]{2,1,0:T(8,128)(2,1)S(1)}, s32[2,8]{1,0:T(2,128)S(1)}, s32[8,128]{1,0:T(8,128)S(1)}, bf16[272,1024]{1,0:T(8,128)(2,1)S(1)}, bf16[144,288]{1,0:T(8,128)(2,1)S(1)}) custom-call(bf16[6,2,2048]{2,1,0:T(2,128)(2,1)} %bitcast.15, s32[2,8]{1,0:T(2,128)} %bitcast.16, s32[1]{0:T(128)S(6)} %copy.6.count_ref, ...), custom_call_target="tpu_custom_call" | custom-call | tf_op jit(solution)/shard_map/pallas_call | solution.py:281
  2.5 0.0 collective-permute-done
  2.5 13.0 %all_to_all.10 = bf16[16,48,128]{2,1,0:T(8,128)(2,1)S(1)} all-to-all(bf16[16,48,128]{2,1,0:T(8,128)(2,1)S(1)} %get-tuple-element.16), channel_id=1, replica_groups={{13,15,9,11,12,14,8,10,5,7,1,3,4,6,0,2},{29,31,25,27,28,30,24,26,21,23,..., dimensions={0} | all-to-all | bytes 393216 | tf_op jit(solution)/shard_map/all_to_all | solution.py:305
  15.5 0.9 %shard_map.56 = bf16[8,144,128]{2,1,0:T(8,128)(2,1)S(1)} custom-call(s32[2,8]{1,0:T(2,128)S(1)} %get-tuple-element.13.mine_ref, s32[2,8]{1,0:T(2,128)S(1)} %bitcast.14, bf16[2,8,2,24,128]{4,3,2,1,0:T(8,128)(2,1)S(1)} %bitcast.13), custom_call_target="tpu_custom_call" | custom-call | tf_op jit(solution)/shard_map/pallas_call | solution.py:307
  16.4 8.6 %all_to_all.11 = bf16[8,144,128]{2,1,0:T(8,128)(2,1)S(1)} all-to-all(bf16[8,144,128]{2,1,0:T(8,128)(2,1)S(1)} %shard_map.56), channel_id=1, replica_groups={{25,24,17,16,9,8,1,0},{27,26,19,18,11,10,3,2},{29,28,21,20,13,12,5,4},{..., dimensions={0} | all-to-all | bytes 589824 | tf_op jit(solution)/shard_map/all_to_all | solution.py:318
  25.0 1.3 %shard_map.57 = bf16[3,3,2,4096]{3,2,1,0:T(2,128)(2,1)} custom-call(s32[8,128]{1,0:T(8,128)S(1)} %get-tuple-element.12.live_ref, bf16[2,576,128]{2,1,0:T(8,128)(2,1)S(1)} %bitcast.12, bf16[272,1024]{1,0:T(8,128)(2,1)S(1)} %get-tuple-element.17.first_ref, bf16[144,288]{1,0:T(8,128)(2,1)S(1)} %get-tuple-element.18.second_ref), custom_call_target="tpu_custom_call" | custom-call | tf_op jit(solution)/shard_map/pallas_call | solution.py:320
Async XLA Ops:
  0.0 2.5 %collective-permute-start = (s32[1,8,2]{1,2,0:T(2,128)}, s32[1,8,2]{1,2,0:T(2,128)S(1)}, u32[]{:S(2)}, u32[]{:S(2)}) collective-permute-start(s32[1,8,2]{1,2,0:T(2,128)} %param.6), channel_id=1, source_target_pairs={{0,1},{1,0},{2,3},{3,2},{4,5},{5,4},{6,7},{7,6},{8,9},{9,8},{10,11... | collective-permute-start | bytes 200 | tf_op jit(solution)/shard_map/ppermute | solution.py:274

commit v6 on v3

--- a/solution.py
+++ b/solution.py
@@ -13,6 +13,8 @@
 LANES = 128
 PARTS = 3
 SLAB = 8
+
+CORES = 2
 
 epsilon = 1e-05
 MESH_AXES = ("tm", "sta")
@@ -36,13 +38,13 @@
 
 
 def whiten_kernel(
-    owners, shards, segments, spectra_ref, pairs_ref, count_ref, *refs
+    classes, shards, segments, spectra_ref, pairs_ref, count_ref, *refs
 ):
-    first_ref, second_ref, o_ref, mine_ref, live_ref, first_held, second_held, x_ref, rows, sems = refs
+    first_ref, second_ref, o_ref, first_held, second_held, x_ref, rows, pairs, sems = refs
     bins = x_ref.shape[2]
     tiles = bins // LANES
     moves = [(spectra_ref.at[pl.ds(g * PARTS, PARTS)], x_ref.at[pl.ds(g * PARTS, PARTS)]) for g in range(segments)]
-    moves += [(pairs_ref, mine_ref), (first_ref, first_held), (second_ref, second_held)]
+    moves += [(pairs_ref, pairs), (first_ref, first_held), (second_ref, second_held)]
     copies = [pltpu.make_async_copy(*move, sems.at[n]) for n, move in enumerate(moves)]
     for copy in copies:
         copy.start()
@@ -94,48 +96,80 @@
                     mixed = pltpu.roll(mixed, LANES - d, 1)
                 rows[d, first : first + 2 * PARTS] = mixed[: 2 * PARTS]
     packed = rows[...].astype(jnp.bfloat16)
-    for device, d in enumerate(owners):
-        o_ref[device] = packed[d]
     for copy in copies[segments:]:
         copy.wait()
-    live_ref[...] = jnp.full(live_ref.shape, count_ref[0])
-
-
-def station_columns(pair_refs, hours, share):
-    near = len(pair_refs)
-    rows = share * hours * near
-    lane = lax.broadcasted_iota(jnp.int32, (rows, hours * share), 1)
-    row = lax.broadcasted_iota(jnp.int32, (rows, hours * share), 0)
-    owner = row % near
-    slot = row // near % hours * share + row // (near * hours)
-    second = lax.axis_index("sta") % near == 1
+    slots = pairs.shape[1]
+    lists = jnp.concatenate([pairs[...].astype(jnp.float32), jnp.zeros((2, LANES - slots), jnp.float32)], axis=1)
+    counts = jnp.full((SLAB - 2, LANES), count_ref[0].astype(jnp.float32))
+    lists = jnp.concatenate([lists, counts], axis=0).astype(jnp.bfloat16)
+    lines = rows.shape[1]
+    for place, d in enumerate(classes):
+        o_ref[place, :lines] = packed[d]
+        o_ref[place, lines:] = lists
+
+
+def station_columns(lists, hours, share):
+    near = len(lists)
+    group = hours * near
+    rows = share * group
+    lane = lax.broadcasted_iota(jnp.int32, (rows, LANES), 1)
+    row = lax.broadcasted_iota(jnp.int32, (rows, LANES), 0)
+    place = group - 1 - row % group
+    owner = place // (hours * CORES) * CORES + place % CORES
+    slot = place // CORES % hours * share + row // group
     columns = []
-    for side in range(2):
-        mine, other = [jnp.broadcast_to(ref[side : side + 1], lane.shape) for ref in pair_refs]
-        lists = [jnp.where(second, other, mine), jnp.where(second, mine, other)]
-        value = jnp.where(owner == 1, lists[1], lists[0])
-        columns.append(jnp.sum(jnp.where(lane == slot, value, 0), axis=1, keepdims=True))
-    return columns
-
-
-def cross_kernel(segments, share, mine_ref, other_ref, w_ref, o_ref, rows):
-    hours, depth, _ = w_ref.shape
+    for side in range(3):
+        value = jnp.broadcast_to(lists[0][side : side + 1], lane.shape)
+        for n in range(1, near):
+            value = jnp.where(owner == n, lists[n][side : side + 1], value)
+        columns.append(jnp.sum(jnp.where(lane == slot, value, 0.0), axis=1, keepdims=True).astype(jnp.int32))
+    live = slot[:, :1] < columns[2]
+    return [jnp.where(live, column, -1) for column in columns[:2]]
+
+
+def first_order(hours, stations):
+    chips = stations // CORES
+    middle = chips // 2
+    along = [*range(middle, -1, -1), *range(middle + 1, chips)]
+    return [(t, z * CORES + core) for t in reversed(range(hours)) for z in along for core in reversed(range(CORES))]
+
+
+def second_order(hours, near):
+    order = [(t, z * CORES + core) for z in range(near // CORES) for t in range(hours) for core in range(CORES)]
+    return order[::-1]
+
+
+def cross_kernel(segments, share, near, w_ref, o_ref, rows):
+    hours, stations, lines, _ = w_ref.shape
+    blocks = lines - SLAB
+    depth = stations * blocks
     group, chunk, _ = o_ref.shape
     slots = group * share
-    kinds = 2 * PARTS
     halves = chunk // (share * PARTS * PARTS * 2)
-    blocks = segments * halves * kinds
+    place_of = [station for _, station in first_order(1, stations)]
+    place_of = [place_of.index(station) for station in range(stations)]
+    cluster = lax.axis_index("sta") // near
+    lists = []
+    for n in range(near):
+        place = 0
+        for m in range(stations // near):
+            place = jnp.where(cluster == m, place_of[m * near + n], place)
+        lists.append(w_ref[0, pl.ds(place, 1), blocks:].reshape(SLAB, LANES).astype(jnp.float32))
     column = lax.broadcasted_iota(jnp.int32, (slots, depth), 1)
     sides = []
-    for station in station_columns((mine_ref, other_ref), hours, share):
-        offset = column - station * blocks
+    for station in station_columns(lists, group // near, share):
+        first = jnp.full(station.shape, depth)
+        for m in range(stations):
+            first = jnp.where(station == m, place_of[m] * blocks, first)
+        offset = column - first
         sides.append([(offset == r).astype(jnp.bfloat16) for r in range(blocks)])
     chosen = jnp.concatenate(sides[0] + sides[1], axis=0)
+    columns = [w_ref[h, :, :blocks].reshape(depth, LANES) for h in range(hours)]
     picked = []
-    for h in range(0, hours, 2):
-        two = jnp.concatenate([w_ref[e] for e in range(h, min(h + 2, hours))], axis=1)
+    for m in range(0, len(columns), 2):
+        two = jnp.concatenate(columns[m : m + 2], axis=1)
         two = jnp.dot(chosen, two, preferred_element_type=jnp.float32)
-        picked += [two[:, e : e + LANES] for e in range(0, two.shape[1], LANES)]
+        picked += [two[:, n : n + LANES] for n in range(0, two.shape[1], LANES)]
 
     def part(side, h, g, j, c, x):
         first = (side * blocks + ((g * halves + j) * PARTS + x) * 2 + c) * slots
@@ -163,14 +197,15 @@
     o_ref[...] = rows[...].reshape(o_ref.shape).astype(jnp.bfloat16)
 
 
-def lag_kernel(live_ref, d_ref, first_ref, second_ref, o_ref, rows, lags_ref, sems):
+def lag_kernel(shards, d_ref, first_ref, second_ref, o_ref, rows, lags_ref, sems):
     share, lags = o_ref.shape[2:]
-    shards = lax.axis_size("tm") * 2
     period = lags // shards
     pieces = period // LANES
-    lines = d_ref.shape[0] // (pieces * shards)
-    total = lines * shards
-    rows[...] = d_ref[...].astype(jnp.float32)
+    chips, hours, depth, _ = d_ref.shape
+    total = chips * depth // pieces
+    lines = total // shards
+    for z in range(chips):
+        rows[z * depth : (z + 1) * depth] = sum(d_ref[z, h].astype(jnp.float32) for h in range(hours))
     daily = []
     for k in range(pieces):
         column = [rows[pl.ds(r * pieces + k, shards, stride=lines * pieces), :] for r in range(lines)]
@@ -191,14 +226,11 @@
         ],
         axis=0,
     )
-    live = live_ref[:1, :1] - lax.axis_index("tm") * share
     cuts = sems.shape[0]
     depth = total // cuts
-    slot = lax.broadcasted_iota(jnp.int32, (depth, period), 0) % share
     copies = []
     for cut in range(cuts):
         joined = jnp.dot(second_ref[cut * depth : (cut + 1) * depth], turned, preferred_element_type=jnp.float32)
-        joined = jnp.where(slot < live, joined, 0.0)
         base = cut * (lags // cuts)
         for a in range(shards // cuts):
             for n in range(PARTS * PARTS):
@@ -240,30 +272,23 @@
     _, _, segments, parts, _, bins = spectra.shape
     slots = pair_blocks.shape[1]
     hours, stations = lax.axis_size("tm"), lax.axis_size("sta")
-    near = 2
-    shards = hours * near
+    near = 2 * CORES if stations % (2 * CORES) == 0 else CORES
+    early = 2 if hours % 2 == 0 else 1
+    late = hours // early
+    shards = late * near
     share = slots // hours
     run = bins // shards
     halves = run // LANES
     chunk_in = segments * halves * 2 * parts
     chunk_out = share * parts * parts * 2 * halves
-
-    def shard(t, s):
-        return t * near + s % near
-
-    swap = [(s, s ^ 1) for s in range(stations)]
-    pairs = pair_blocks[0].T
-    other = lax.ppermute(pair_blocks, "sta", swap)[0].T
-    depth = stations * chunk_in
-
-    owners = [shard(t, s) for t in range(hours) for s in range(stations)]
+    order = first_order(late, stations)
+    shard_of = second_order(late, near)
+    classes = [shard_of.index((t, s % near)) for t, s in order]
     first, second = lag_tables(bins, shards, share)
-    white, mine, live, first, second = kernel_call(
-        functools.partial(whiten_kernel, owners, shards, segments),
+    white, first, second = kernel_call(
+        functools.partial(whiten_kernel, classes, shards, segments),
         (
-            pltpu.VMEM((hours * stations, chunk_in, LANES), jnp.bfloat16),
-            pltpu.VMEM((2, slots), jnp.int32),
-            pltpu.VMEM((SLAB, LANES), jnp.int32),
+            pltpu.VMEM((late * stations, chunk_in + SLAB, LANES), jnp.bfloat16),
             pltpu.VMEM(first.shape, first.dtype),
             pltpu.VMEM(second.shape, second.dtype),
         ),
@@ -271,41 +296,41 @@
         [
             pltpu.VMEM((segments * parts, 2, bins), jnp.bfloat16),
             pltpu.VMEM((shards, chunk_in, LANES), jnp.float32),
+            pltpu.VMEM((2, slots), jnp.int32),
             pltpu.SemaphoreType.DMA((segments + 3,)),
         ],
     )(
         in_hbm(spectra.reshape(segments * parts, 2, bins)),
-        in_hbm(pairs),
+        in_hbm(pair_blocks[0].T),
         block_count,
         in_hbm(first),
         in_hbm(second),
     )
-    white, other = lax.optimization_barrier((white, other))
-    every = lax.all_to_all(white, MESH_AXES, 0, 0, tiled=True)
+    groups = [[(h * late + t) * stations + s for t, s in order] for h in range(early)]
+    every = lax.all_to_all(white, MESH_AXES, 0, 0, tiled=True, axis_index_groups=groups)
 
     daily = kernel_call(
-        functools.partial(cross_kernel, segments, share),
-        pltpu.VMEM((shards, chunk_out, LANES), jnp.bfloat16),
+        functools.partial(cross_kernel, segments, share, near),
+        pltpu.VMEM((hours * near, chunk_out, LANES), jnp.bfloat16),
+        [VMEM],
+        [pltpu.VMEM((hours * near * chunk_out, LANES), jnp.float32)],
+    )(every.reshape(late, stations, chunk_in + SLAB, LANES))
+
+    order = second_order(hours, near)
+    groups = [[t * stations + s + m for t, m in order] for s in range(0, stations, near)]
+    whole = lax.all_to_all(daily, MESH_AXES, 0, 0, tiled=True, axis_index_groups=groups)
+
+    result = kernel_call(
+        functools.partial(lag_kernel, shards),
+        jax.ShapeDtypeStruct((parts, parts, share, 2 * bins), jnp.bfloat16),
         [VMEM] * 3,
-        [pltpu.VMEM((shards * chunk_out, LANES), jnp.float32)],
-    )(mine, other, every.reshape(hours, depth, LANES))
-
-    groups = [
-        [t * stations + s + e for t in range(hours) for e in range(near)] for s in range(0, stations, near)
-    ]
-    whole = lax.all_to_all(daily, MESH_AXES, 0, 0, tiled=True, axis_index_groups=groups)
-
-    result = kernel_call(
-        lag_kernel,
-        jax.ShapeDtypeStruct((parts, parts, share, 2 * bins), jnp.bfloat16),
-        [VMEM] * 4,
         [
             pltpu.VMEM((shards * chunk_out, LANES), jnp.float32),
             pltpu.VMEM((parts, parts, share, 2 * bins), jnp.bfloat16),
             pltpu.SemaphoreType.DMA((2,)),
         ],
         pl.BlockSpec(memory_space=pl.ANY),
-    )(live, whole.reshape(shards * chunk_out, LANES), first, second)
+    )(whole.reshape(near // CORES, early, late * CORES * chunk_out, LANES), first, second)
     return result.transpose(2, 0, 1, 3).reshape(1, share, 1, 1, parts, parts, 2 * bins)
 
 

time: 28.4 us -> 25.2 us (0.89)
  blocking collectives: 23.7 us -> 20.9 us
  starting transfers between devices: 0.45 us -> 0 us
    all_to_all x1, blocking collectives: 15.5 us -> 11.4 us  [body(): lax.all_to_all(white, MESH_AXES, 0, 0, tiled=True, axis_index_groups=groups)]
    all_to_all x1, blocking collectives: 8.19 us -> 9.47 us  [body(): lax.all_to_all(daily, MESH_AXES, 0, 0, tiled=True, axis_index_groups=groups)]
    ppermute x1 -> x0, starting transfers between devices: 0.45 us -> none  [body(): other = lax.ppermute(pair_blocks, 'sta', swap)[0].T]
  transfers between devices with their start and end apart: 1 -> 0, of which waited for: 0 -> 0; matrix products, arithmetic and copies ran while one was open for 0% -> 0% of each run, Pallas kernels for 5% -> 0%
where the time goes in v6:
time: 25.2 us; the launch traced here: 24.9 us
  blocking collectives  20.9 us (83%)
  Pallas kernels  3.4 us (13%)
  between operations  0.67 us (3%)
    all_to_all x1, blocking collectives, body(): lax.all_to_all(white, MESH_AXES, 0, 0, tiled=True, axis_index_groups=groups)  11.4 us
    all_to_all x1, blocking collectives, body(): lax.all_to_all(daily, MESH_AXES, 0, 0, tiled=True, axis_index_groups=groups)  9.47 us
    pallas_call x1, Pallas kernels, body(): kernel_call(functools.partial(whiten_kernel, classes, shards, segments),...  1.34 us
    pallas_call x1, Pallas kernels, body(): kernel_call(functools.partial(lag_kernel, shards), jax.ShapeDtypeStruct((...  1.27 us
    pallas_call x1, Pallas kernels, body(): kernel_call(functools.partial(cross_kernel, segments, share, near), pltpu...  0.79 us

profile of v6, /device:TPU:0, one launch (start us, length us, event | category | flops | bytes accessed | tf_op | source)
XLA Modules:
  0.0 24.9 jit_solution(15899872046397176192)
XLA Ops:
  0.7 1.3 %shard_map.55 = (bf16[16,32,128]{2,1,0:T(8,128)(2,1)S(1)}, bf16[272,1024]{1,0:T(8,128)(2,1)S(1)}, bf16[144,288]{1,0:T(8,128)(2,1)S(1)}) custom-call(bf16[6,2,2048]{2,1,0:T(2,128)(2,1)} %bitcast.11, s32[2,8]{1,0:T(2,128)} %bitcast.12, s32[1]{0:T(128)S(6)} %copy.6.count_ref, bf16[272,1024]{1,0:T(8,128)(2,1)} %constant.4.clone.refs_0_, ...), custom_call_target="tpu_custom_call" | custom-call | tf_op jit(solution)/shard_map/pallas_call | solution.py:288
  2.0 11.4 %all_to_all.10 = bf16[16,32,128]{2,1,0:T(8,128)(2,1)S(1)} all-to-all(bf16[16,32,128]{2,1,0:T(8,128)(2,1)S(1)} %get-tuple-element.8), channel_id=1, replica_groups={{13,12,11,10,9,8,15,14,5,4,3,2,1,0,7,6},{29,28,27,26,25,24,31,30,21,20,..., dimensions={0} | all-to-all | bytes 262144 | tf_op jit(solution)/shard_map/all_to_all | solution.py:310
  13.4 0.8 %shard_map.56 = bf16[16,72,128]{2,1,0:T(8,128)(2,1)S(1)} custom-call(bf16[2,8,32,128]{3,2,1,0:T(8,128)(2,1)S(1)} %bitcast.10), custom_call_target="tpu_custom_call" | custom-call | tf_op jit(solution)/shard_map/pallas_call | solution.py:312
  14.2 9.5 %all_to_all.11 = bf16[16,72,128]{2,1,0:T(8,128)(2,1)S(1)} all-to-all(bf16[16,72,128]{2,1,0:T(8,128)(2,1)S(1)} %shard_map.56), channel_id=1, replica_groups={{27,26,19,18,11,10,3,2,25,24,17,16,9,8,1,0},{31,30,23,22,15,14,7,6,29,2..., dimensions={0} | all-to-all | bytes 589824 | tf_op jit(solution)/shard_map/all_to_all | solution.py:321
  23.7 1.3 %shard_map.57 = bf16[3,3,2,4096]{3,2,1,0:T(2,128)(2,1)} custom-call(bf16[2,2,288,128]{3,2,1,0:T(8,128)(2,1)S(1)} %bitcast.9, bf16[272,1024]{1,0:T(8,128)(2,1)S(1)} %get-tuple-element.9.first_ref, bf16[144,288]{1,0:T(8,128)(2,1)S(1)} %get-tuple-element.10.second_ref), custom_call_target="tpu_custom_call" | custom-call | tf_op jit(solution)/shard_map/pallas_call | solution.py:323

commit v7 on v6

--- a/solution.py
+++ b/solution.py
@@ -19,45 +19,43 @@
 epsilon = 1e-05
 MESH_AXES = ("tm", "sta")
 VMEM = pl.BlockSpec(memory_space=pltpu.VMEM)
-HBM = pl.BlockSpec(memory_space=pltpu.HBM)
-
-
-def in_hbm(array):
-    return pltpu.with_memory_space_constraint(array, pltpu.HBM)
-
-
-def kernel_call(kernel, out_shape, in_specs, scratch, out_spec=VMEM):
+
+
+placed = pltpu.with_memory_space_constraint
+
+
+def kernel_call(kernel, out_shape, in_specs, scratch, out_spec=VMEM, weight=1):
     return pl.pallas_call(
         kernel,
         out_shape=out_shape,
         in_specs=in_specs,
         out_specs=jax.tree.map(lambda _: out_spec, out_shape),
         scratch_shapes=scratch,
+        cost_estimate=pl.CostEstimate(flops=weight * 10**9, bytes_accessed=weight * 4 * 10**6, transcendentals=0),
         compiler_params=pltpu.CompilerParams(vmem_limit_bytes=40 * 1024 * 1024),
     )
 
 
+def band_kernel(o_ref):
+    apart = lax.broadcasted_iota(jnp.int32, (3 * LANES, LANES), 0) - LANES
+    apart = apart - lax.broadcasted_iota(jnp.int32, (3 * LANES, LANES), 1)
+    o_ref[...] = (jnp.abs(apart) <= SMOOTH).astype(jnp.bfloat16)
+
+
 def whiten_kernel(
-    classes, shards, segments, spectra_ref, pairs_ref, count_ref, *refs
+    classes, shards, segments, x_ref, pairs_ref, count_ref, band_ref, o_ref, rows, pairs, sem
 ):
-    first_ref, second_ref, o_ref, first_held, second_held, x_ref, rows, pairs, sems = refs
+    pairs_copy = pltpu.make_async_copy(pairs_ref, pairs, sem)
+    pairs_copy.start()
     bins = x_ref.shape[2]
     tiles = bins // LANES
-    moves = [(spectra_ref.at[pl.ds(g * PARTS, PARTS)], x_ref.at[pl.ds(g * PARTS, PARTS)]) for g in range(segments)]
-    moves += [(pairs_ref, pairs), (first_ref, first_held), (second_ref, second_held)]
-    copies = [pltpu.make_async_copy(*move, sems.at[n]) for n, move in enumerate(moves)]
-    for copy in copies:
-        copy.start()
     lane = lax.broadcasted_iota(jnp.int32, (SLAB, LANES), 1)
     even = lax.broadcasted_iota(jnp.int32, (SLAB, LANES), 0) % 2 == 0
     turn = [lane % shards == k for k in range(shards)]
     blank = jnp.zeros((SLAB, LANES), jnp.float32)
-    apart = lax.broadcasted_iota(jnp.int32, (3 * LANES, LANES), 0) - LANES
-    apart = apart - lax.broadcasted_iota(jnp.int32, (3 * LANES, LANES), 1)
-    band = (jnp.abs(apart) <= SMOOTH).astype(jnp.bfloat16)
+    band = band_ref[...]
     values, blocks = [], []
     for g in range(segments):
-        copies[g].wait()
         lines = [x_ref[g * PARTS + x].astype(jnp.float32) for x in range(PARTS)]
         lines = jnp.concatenate(lines + [jnp.zeros((SLAB - 2 * PARTS, bins), jnp.float32)], axis=0)
         value = [lines[:, v * LANES : (v + 1) * LANES] for v in range(tiles)]
@@ -96,8 +94,7 @@
                     mixed = pltpu.roll(mixed, LANES - d, 1)
                 rows[d, first : first + 2 * PARTS] = mixed[: 2 * PARTS]
     packed = rows[...].astype(jnp.bfloat16)
-    for copy in copies[segments:]:
-        copy.wait()
+    pairs_copy.wait()
     slots = pairs.shape[1]
     lists = jnp.concatenate([pairs[...].astype(jnp.float32), jnp.zeros((2, LANES - slots), jnp.float32)], axis=1)
     counts = jnp.full((SLAB - 2, LANES), count_ref[0].astype(jnp.float32))
@@ -115,8 +112,8 @@
     lane = lax.broadcasted_iota(jnp.int32, (rows, LANES), 1)
     row = lax.broadcasted_iota(jnp.int32, (rows, LANES), 0)
     place = group - 1 - row % group
-    owner = place // (hours * CORES) * CORES + place % CORES
-    slot = place // CORES % hours * share + row // group
+    owner = place // hours % (near // CORES) * CORES + place // (hours * (near // CORES))
+    slot = place % hours * share + row // group
     columns = []
     for side in range(3):
         value = jnp.broadcast_to(lists[0][side : side + 1], lane.shape)
@@ -135,7 +132,7 @@
 
 
 def second_order(hours, near):
-    order = [(t, z * CORES + core) for z in range(near // CORES) for t in range(hours) for core in range(CORES)]
+    order = [(t, z * CORES + core) for core in range(CORES) for z in range(near // CORES) for t in range(hours)]
     return order[::-1]
 
 
@@ -201,11 +198,11 @@
     share, lags = o_ref.shape[2:]
     period = lags // shards
     pieces = period // LANES
-    chips, hours, depth, _ = d_ref.shape
-    total = chips * depth // pieces
+    members, hours, depth, _ = d_ref.shape
+    total = members * depth // pieces
     lines = total // shards
-    for z in range(chips):
-        rows[z * depth : (z + 1) * depth] = sum(d_ref[z, h].astype(jnp.float32) for h in range(hours))
+    for m in range(members):
+        rows[m * depth : (m + 1) * depth] = sum(d_ref[m, h].astype(jnp.float32) for h in range(hours))
     daily = []
     for k in range(pieces):
         column = [rows[pl.ds(r * pieces + k, shards, stride=lines * pieces), :] for r in range(lines)]
@@ -285,26 +282,22 @@
     shard_of = second_order(late, near)
     classes = [shard_of.index((t, s % near)) for t, s in order]
     first, second = lag_tables(bins, shards, share)
-    white, first, second = kernel_call(
+    band = kernel_call(band_kernel, pltpu.VMEM((3 * LANES, LANES), jnp.bfloat16), [], [], weight=4)()
+    band, block_count = lax.optimization_barrier((band, block_count))
+    white = kernel_call(
         functools.partial(whiten_kernel, classes, shards, segments),
-        (
-            pltpu.VMEM((late * stations, chunk_in + SLAB, LANES), jnp.bfloat16),
-            pltpu.VMEM(first.shape, first.dtype),
-            pltpu.VMEM(second.shape, second.dtype),
-        ),
-        [HBM, HBM, pl.BlockSpec(memory_space=pltpu.SMEM), HBM, HBM],
+        pltpu.VMEM((late * stations, chunk_in + SLAB, LANES), jnp.bfloat16),
+        [VMEM, pl.BlockSpec(memory_space=pltpu.HBM), pl.BlockSpec(memory_space=pltpu.SMEM), VMEM],
         [
-            pltpu.VMEM((segments * parts, 2, bins), jnp.bfloat16),
             pltpu.VMEM((shards, chunk_in, LANES), jnp.float32),
             pltpu.VMEM((2, slots), jnp.int32),
-            pltpu.SemaphoreType.DMA((segments + 3,)),
+            pltpu.SemaphoreType.DMA,
         ],
     )(
-        in_hbm(spectra.reshape(segments * parts, 2, bins)),
-        in_hbm(pair_blocks[0].T),
+        placed(spectra.reshape(segments * parts, 2, bins), pltpu.VMEM),
+        placed(pair_blocks[0].T, pltpu.HBM),
         block_count,
-        in_hbm(first),
-        in_hbm(second),
+        band,
     )
     groups = [[(h * late + t) * stations + s for t, s in order] for h in range(early)]
     every = lax.all_to_all(white, MESH_AXES, 0, 0, tiled=True, axis_index_groups=groups)
@@ -330,16 +323,16 @@
             pltpu.SemaphoreType.DMA((2,)),
         ],
         pl.BlockSpec(memory_space=pl.ANY),
-    )(whole.reshape(near // CORES, early, late * CORES * chunk_out, LANES), first, second)
+    )(whole.reshape(near, early, late * chunk_out, LANES), first, second)
     return result.transpose(2, 0, 1, 3).reshape(1, share, 1, 1, parts, parts, 2 * bins)
 
 
 def solution(mesh):
-    placed = (P("tm", "sta", None, None, None, None), P("sta", None, None), P("sta"))
+    specs = (P("tm", "sta", None, None, None, None), P("sta", None, None), P("sta"))
     return jax.shard_map(
         body,
         mesh=mesh,
-        in_specs=placed,
+        in_specs=specs,
         out_specs=P("sta", "tm", None, None, None, None, None),
         check_vma=False,
     )

time: 25.2 us -> 24.6 us (0.976)
  Pallas kernels: 3.4 us -> 2.8 us
    pallas_call x1, Pallas kernels: 1.34 us -> 0.7 us  [body(): kernel_call(functools.partial(whiten_kernel, classes, shards, segments),...]
where the time goes in v7:
time: 24.6 us; the launch traced here: 24.4 us
  blocking collectives  20.8 us (85%)
  Pallas kernels  2.8 us (11%)
  between operations  0.68 us (3%)
    all_to_all x1, blocking collectives, body(): lax.all_to_all(white, MESH_AXES, 0, 0, tiled=True, axis_index_groups=groups)  11.4 us
    all_to_all x1, blocking collectives, body(): lax.all_to_all(daily, MESH_AXES, 0, 0, tiled=True, axis_index_groups=groups)  9.37 us
    pallas_call x1, Pallas kernels, body(): kernel_call(functools.partial(lag_kernel, shards), jax.ShapeDtypeStruct((...  1.27 us
    pallas_call x1, Pallas kernels, body(): kernel_call(functools.partial(cross_kernel, segments, share, near), pltpu...  0.79 us
    pallas_call x1, Pallas kernels, body(): kernel_call(functools.partial(whiten_kernel, classes, shards, segments),...  0.7 us

profile of v7, /device:TPU:0, one launch (start us, length us, event | category | flops | bytes accessed | tf_op | source)
XLA Modules:
  0.0 24.4 jit_solution(9761573182738541844)
XLA Ops:
  0.0 0.0 copy-start
  0.7 0.1 copy-done
  0.8 0.7 %shard_map.56 = bf16[16,32,128]{2,1,0:T(8,128)(2,1)S(1)} custom-call(bf16[6,2,2048]{2,1,0:T(2,128)(2,1)S(1)} %bitcast.11, s32[2,8]{1,0:T(2,128)} %bitcast.12, s32[1]{0:T(128)S(6)} %copy.6.count_ref, bf16[384,128]{1,0:T(8,128)(2,1)S(1)} %shard_map.55.band_ref), custom_call_target="tpu_custom_call" | custom-call | flops 1000000000 | bytes 4000000 | tf_op jit(solution)/shard_map/pallas_call | solution.py:287
  1.5 11.4 %all_to_all.10 = bf16[16,32,128]{2,1,0:T(8,128)(2,1)S(1)} all-to-all(bf16[16,32,128]{2,1,0:T(8,128)(2,1)S(1)} %shard_map.56), channel_id=1, replica_groups={{13,12,11,10,9,8,15,14,5,4,3,2,1,0,7,6},{29,28,27,26,25,24,31,30,21,20,..., dimensions={0} | all-to-all | bytes 262144 | tf_op jit(solution)/shard_map/all_to_all | solution.py:303
  12.9 0.0 copy-start.2
  12.9 0.8 %shard_map.57 = bf16[16,72,128]{2,1,0:T(8,128)(2,1)S(1)} custom-call(bf16[2,8,32,128]{3,2,1,0:T(8,128)(2,1)S(1)} %bitcast.10), custom_call_target="tpu_custom_call" | custom-call | flops 1000000000 | bytes 4000000 | tf_op jit(solution)/shard_map/pallas_call | solution.py:305
  13.7 0.0 copy-start.1
  13.7 9.4 %all_to_all.11 = bf16[16,72,128]{2,1,0:T(8,128)(2,1)S(1)} all-to-all(bf16[16,72,128]{2,1,0:T(8,128)(2,1)S(1)} %shard_map.57), channel_id=1, replica_groups={{27,19,11,3,25,17,9,1,26,18,10,2,24,16,8,0},{31,23,15,7,29,21,13,5,30,2..., dimensions={0} | all-to-all | bytes 589824 | tf_op jit(solution)/shard_map/all_to_all | solution.py:314
  23.1 0.0 copy-done.2
  23.1 0.0 copy-done.1
  23.1 1.3 %shard_map.58 = bf16[3,3,2,4096]{3,2,1,0:T(2,128)(2,1)} custom-call(bf16[4,2,144,128]{3,2,1,0:T(8,128)(2,1)S(1)} %bitcast.9, bf16[272,1024]{1,0:T(8,128)(2,1)S(1)} %copy-done.1, bf16[144,288]{1,0:T(8,128)(2,1)S(1)} %copy-done.2), custom_call_target="tpu_custom_call" | custom-call | flops 1000000000 | bytes 4000000 | tf_op jit(solution)/shard_map/pallas_call | solution.py:316
  (1 shorter events, 0.0 us)
Async XLA Ops:
  0.0 0.8 %copy-start = (bf16[1,1,2,3,2,2048]{5,4,3,2,1,0:T(2,128)(2,1)S(1)}, bf16[1,1,2,3,2,2048]{5,4,3,2,1,0:T(2,128)(2,1)}, u32[]{:S(2)}) copy-start(bf16[1,1,2,3,2,2048]{5,4,3,2,1,0:T(2,128)(2,1)} %param.5) | copy-start | bytes 147460
  12.9 10.2 %copy-start.2 = (bf16[144,288]{1,0:T(8,128)(2,1)S(1)}, bf16[144,288]{1,0:T(8,128)(2,1)}, u32[]{:S(2)}) copy-start(bf16[144,288]{1,0:T(8,128)(2,1)} %constant.5.clone.second_ref) | copy-start | bytes 248836
  13.7 9.4 %copy-start.1 = (bf16[272,1024]{1,0:T(8,128)(2,1)S(1)}, bf16[272,1024]{1,0:T(8,128)(2,1)}, u32[]{:S(2)}) copy-start(bf16[272,1024]{1,0:T(8,128)(2,1)} %constant.4.clone.first_ref) | copy-start | bytes 1671172

commit v8 on v7

--- a/solution.py
+++ b/solution.py
@@ -189,62 +189,78 @@
         for n in range(PARTS * PARTS):
             for c, total in enumerate((real[n], imag[n])):
                 for u in range(share):
-                    row = ((u * PARTS * PARTS + n) * 2 + c) * halves + j
+                    row = ((n * share + u) * 2 + c) * halves + j
                     rows[pl.ds(row, group, stride=chunk), :] = total[u * group : (u + 1) * group]
     o_ref[...] = rows[...].reshape(o_ref.shape).astype(jnp.bfloat16)
 
 
-def lag_kernel(shards, d_ref, first_ref, second_ref, o_ref, rows, lags_ref, sems):
-    share, lags = o_ref.shape[2:]
-    period = lags // shards
+def real_sums(re, im):
+    n = len(re)
+    if n == 1:
+        return re
+    half = n // 2
+    even, odd = [], []
+    for d in range(half):
+        even.append((re[d] + re[d + half], im[d] + im[d + half]))
+        x, y = re[d] - re[d + half], im[d] - im[d + half]
+        if d == 0:
+            odd.append((x, y))
+        elif 4 * d == n:
+            odd.append((-y, x))
+        else:
+            cos, sin = math.cos(2.0 * math.pi * d / n), math.sin(2.0 * math.pi * d / n)
+            odd.append((x * cos - y * sin, x * sin + y * cos))
+    sums = [real_sums(*map(list, zip(*values))) for values in (even, odd)]
+    return [sums[a % 2][a // 2] for a in range(n)]
+
+
+def lag_kernel(shards, share, d_ref, table_ref, o_ref, rows, lags_ref, sem):
+    period = o_ref.shape[3] // shards
     pieces = period // LANES
     members, hours, depth, _ = d_ref.shape
-    total = members * depth // pieces
-    lines = total // shards
+    lines = share * PARTS * PARTS
+    padded = -(-lines // SLAB) * SLAB
     for m in range(members):
         rows[m * depth : (m + 1) * depth] = sum(d_ref[m, h].astype(jnp.float32) for h in range(hours))
+    if padded > lines:
+        rows[members * depth :] = jnp.zeros((rows.shape[0] - members * depth, LANES), jnp.float32)
+    half = pieces // 2
     daily = []
-    for k in range(pieces):
-        column = [rows[pl.ds(r * pieces + k, shards, stride=lines * pieces), :] for r in range(lines)]
-        daily.append(jnp.concatenate(column, axis=0).astype(jnp.bfloat16))
-    half = pieces // 2
-    daily = jnp.concatenate([jnp.concatenate(daily[c * half : (c + 1) * half], axis=1) for c in range(2)], axis=0)
+    for c in range(2):
+        for d in range(shards):
+            first = d * lines * pieces + c * half
+            line = [rows[pl.ds(first + j, padded, stride=pieces), :] for j in range(half)]
+            daily.append(jnp.concatenate(line, axis=1))
+    daily = jnp.concatenate(daily, axis=0).astype(jnp.bfloat16)
     run = period // 2
-    middle = jnp.dot(daily, first_ref[:run], preferred_element_type=jnp.float32)
-    re = (middle[:total, :period] - middle[total:, period:]).reshape(lines, shards, period)
-    im = (middle[:total, period:] + middle[total:, :period]).reshape(lines, shards, period)
-    turn = first_ref[run : run + 2 * shards].astype(jnp.float32)
+    middle = jnp.dot(daily, table_ref[:run], preferred_element_type=jnp.float32)
+    turn = table_ref[run : run + 2 * shards].astype(jnp.float32)
     turn = turn[:shards] + turn[shards:]
-    cos, sin = turn[None, :, :period], turn[None, :, period:]
-    turned = jnp.concatenate(
-        [
-            (re * cos - im * sin).reshape(total, period).astype(jnp.bfloat16),
-            (re * sin + im * cos).reshape(total, period).astype(jnp.bfloat16),
-        ],
-        axis=0,
-    )
-    cuts = sems.shape[0]
-    depth = total // cuts
-    copies = []
-    for cut in range(cuts):
-        joined = jnp.dot(second_ref[cut * depth : (cut + 1) * depth], turned, preferred_element_type=jnp.float32)
-        base = cut * (lags // cuts)
-        for a in range(shards // cuts):
-            for n in range(PARTS * PARTS):
-                first = (a * PARTS * PARTS + n) * share
-                value = joined[first : first + share].astype(jnp.bfloat16)
-                lags_ref[n // PARTS, n % PARTS, :, base + a * period : base + (a + 1) * period] = value
-        window = (slice(None),) * 3 + (pl.ds(base, lags // cuts),)
-        copies.append(pltpu.make_async_copy(lags_ref.at[window], o_ref.at[window], sems.at[cut]))
-        copies[-1].start()
-    for copy in copies:
-        copy.wait()
-
-
-def lag_tables(bins, shards, share):
+    total = shards * padded
+    re, im = [], []
+    for d in range(shards):
+        first = d * padded
+        with_re, with_im = middle[first : first + padded], middle[total + first : total + first + padded]
+        x = with_re[:, :period] - with_im[:, period:]
+        y = with_re[:, period:] + with_im[:, :period]
+        cos, sin = turn[d : d + 1, :period], turn[d : d + 1, period:]
+        re.append(x * cos - y * sin)
+        im.append(x * sin + y * cos)
+    sums = real_sums(re, im)
+    for a in range(shards):
+        value = sums[(a + shards // 2) % shards]
+        for n in range(PARTS * PARTS):
+            lags_ref[n // PARTS, n % PARTS, :, a * period : (a + 1) * period] = value[n * share : (n + 1) * share].astype(
+                jnp.bfloat16
+            )
+    copy = pltpu.make_async_copy(lags_ref, o_ref, sem)
+    copy.start()
+    copy.wait()
+
+
+def lag_table(bins, shards):
     lags = 2 * bins
     period = lags // shards
-    lines = share * PARTS * PARTS
     lane = np.arange(LANES)
     inner = lane % shards * (LANES // shards) + lane // shards
     k = (np.arange(0, bins // shards, LANES)[:, None] + inner).reshape(-1, 1)
@@ -256,13 +272,8 @@
 
     fine = turns(d * b * (2.0 * math.pi / lags)) * bins**-0.5
     high = fine.astype(jnp.bfloat16).astype(np.float64)
-    first = np.concatenate([turns((k * b % period) * (2.0 * math.pi / period)), high, fine - high])
-    a = np.arange(shards)[:, None] - bins // period
-    turn = (a * d.T % shards) * (2.0 * math.pi / shards)
-    same = np.eye(lines).reshape(share, PARTS * PARTS, lines).transpose(1, 0, 2)
-    second = [np.einsum("ad,nur->anurd", table, same) for table in (np.cos(turn), -np.sin(turn))]
-    second = np.concatenate([table.reshape(lines * shards, -1) for table in second], axis=1)
-    return jnp.asarray(first, jnp.bfloat16), jnp.asarray(second, jnp.bfloat16)
+    table = np.concatenate([turns((k * b % period) * (2.0 * math.pi / period)), high, fine - high])
+    return jnp.asarray(table, jnp.bfloat16)
 
 
 def body(spectra, pair_blocks, block_count):
@@ -281,7 +292,6 @@
     order = first_order(late, stations)
     shard_of = second_order(late, near)
     classes = [shard_of.index((t, s % near)) for t, s in order]
-    first, second = lag_tables(bins, shards, share)
     band = kernel_call(band_kernel, pltpu.VMEM((3 * LANES, LANES), jnp.bfloat16), [], [], weight=4)()
     band, block_count = lax.optimization_barrier((band, block_count))
     white = kernel_call(
@@ -313,17 +323,18 @@
     groups = [[t * stations + s + m for t, m in order] for s in range(0, stations, near)]
     whole = lax.all_to_all(daily, MESH_AXES, 0, 0, tiled=True, axis_index_groups=groups)
 
+    overrun = -(share * parts * parts) % SLAB * 2 * halves
     result = kernel_call(
-        functools.partial(lag_kernel, shards),
+        functools.partial(lag_kernel, shards, share),
         jax.ShapeDtypeStruct((parts, parts, share, 2 * bins), jnp.bfloat16),
-        [VMEM] * 3,
+        [VMEM] * 2,
         [
-            pltpu.VMEM((shards * chunk_out, LANES), jnp.float32),
+            pltpu.VMEM((shards * chunk_out + overrun, LANES), jnp.float32),
             pltpu.VMEM((parts, parts, share, 2 * bins), jnp.bfloat16),
-            pltpu.SemaphoreType.DMA((2,)),
+            pltpu.SemaphoreType.DMA,
         ],
         pl.BlockSpec(memory_space=pl.ANY),
-    )(whole.reshape(near, early, late * chunk_out, LANES), first, second)
+    )(whole.reshape(near, early, late * chunk_out, LANES), lag_table(bins, shards))
     return result.transpose(2, 0, 1, 3).reshape(1, share, 1, 1, parts, parts, 2 * bins)
 
 

time: 24.6 us -> 24.5 us (level)
  no operation moved by 1% of the time
where the time goes in v8:
time: 24.5 us; the launch traced here: 24.3 us
  blocking collectives  20.8 us (85%)
  Pallas kernels  2.72 us (11%)
  between operations  0.68 us (3%)
    all_to_all x1, blocking collectives, body(): lax.all_to_all(white, MESH_AXES, 0, 0, tiled=True, axis_index_groups=groups)  11.4 us
    all_to_all x1, blocking collectives, body(): lax.all_to_all(daily, MESH_AXES, 0, 0, tiled=True, axis_index_groups=groups)  9.37 us
    pallas_call x1, Pallas kernels, body(): kernel_call(functools.partial(lag_kernel, shards, share), jax.ShapeDtypeS...  1.19 us
    pallas_call x1, Pallas kernels, body(): kernel_call(functools.partial(cross_kernel, segments, share, near), pltpu...  0.79 us
    pallas_call x1, Pallas kernels, body(): kernel_call(functools.partial(whiten_kernel, classes, shards, segments),...  0.7 us

profile of v8, /device:TPU:0, one launch (start us, length us, event | category | flops | bytes accessed | tf_op | source)
XLA Modules:
  0.0 24.3 jit_solution(8708098783466712270)
XLA Ops:
  0.0 0.0 copy-start
  0.7 0.1 copy-done
  0.8 0.7 %shard_map.47 = bf16[16,32,128]{2,1,0:T(8,128)(2,1)S(1)} custom-call(bf16[6,2,2048]{2,1,0:T(2,128)(2,1)S(1)} %bitcast.11, s32[2,8]{1,0:T(2,128)} %bitcast.12, s32[1]{0:T(128)S(6)} %copy.5.count_ref, bf16[384,128]{1,0:T(8,128)(2,1)S(1)} %shard_map.46.band_ref), custom_call_target="tpu_custom_call" | custom-call | flops 1000000000 | bytes 4000000 | tf_op jit(solution)/shard_map/pallas_call | solution.py:297
  1.5 11.4 %all_to_all.10 = bf16[16,32,128]{2,1,0:T(8,128)(2,1)S(1)} all-to-all(bf16[16,32,128]{2,1,0:T(8,128)(2,1)S(1)} %shard_map.47), channel_id=1, replica_groups={{13,12,11,10,9,8,15,14,5,4,3,2,1,0,7,6},{29,28,27,26,25,24,31,30,21,20,..., dimensions={0} | all-to-all | bytes 262144 | tf_op jit(solution)/shard_map/all_to_all | solution.py:313
  12.9 0.8 %shard_map.48 = bf16[16,72,128]{2,1,0:T(8,128)(2,1)S(1)} custom-call(bf16[2,8,32,128]{3,2,1,0:T(8,128)(2,1)S(1)} %bitcast.10), custom_call_target="tpu_custom_call" | custom-call | flops 1000000000 | bytes 4000000 | tf_op jit(solution)/shard_map/pallas_call | solution.py:315
  13.7 0.0 copy-start.1
  13.7 9.4 %all_to_all.11 = bf16[16,72,128]{2,1,0:T(8,128)(2,1)S(1)} all-to-all(bf16[16,72,128]{2,1,0:T(8,128)(2,1)S(1)} %shard_map.48), channel_id=1, replica_groups={{27,19,11,3,25,17,9,1,26,18,10,2,24,16,8,0},{31,23,15,7,29,21,13,5,30,2..., dimensions={0} | all-to-all | bytes 589824 | tf_op jit(solution)/shard_map/all_to_all | solution.py:324
  23.1 0.0 copy-done.1
  23.1 1.2 %shard_map.49 = bf16[3,3,2,4096]{3,2,1,0:T(2,128)(2,1)} custom-call(bf16[4,2,144,128]{3,2,1,0:T(8,128)(2,1)S(1)} %bitcast.9, bf16[272,1024]{1,0:T(8,128)(2,1)S(1)} %copy-done.1), custom_call_target="tpu_custom_call" | custom-call | flops 1000000000 | bytes 4000000 | tf_op jit(solution)/shard_map/pallas_call | solution.py:327
  (1 shorter events, 0.0 us)
Async XLA Ops:
  0.0 0.8 %copy-start = (bf16[1,1,2,3,2,2048]{5,4,3,2,1,0:T(2,128)(2,1)S(1)}, bf16[1,1,2,3,2,2048]{5,4,3,2,1,0:T(2,128)(2,1)}, u32[]{:S(2)}) copy-start(bf16[1,1,2,3,2,2048]{5,4,3,2,1,0:T(2,128)(2,1)} %param.4) | copy-start | bytes 147460
  13.7 9.4 %copy-start.1 = (bf16[272,1024]{1,0:T(8,128)(2,1)S(1)}, bf16[272,1024]{1,0:T(8,128)(2,1)}, u32[]{:S(2)}) copy-start(bf16[272,1024]{1,0:T(8,128)(2,1)} %constant.2.clone.table_ref) | copy-start | bytes 1671172

commit v9 on v8

--- a/solution.py
+++ b/solution.py
@@ -191,7 +191,7 @@
                 for u in range(share):
                     row = ((n * share + u) * 2 + c) * halves + j
                     rows[pl.ds(row, group, stride=chunk), :] = total[u * group : (u + 1) * group]
-    o_ref[...] = rows[...].reshape(o_ref.shape).astype(jnp.bfloat16)
+    o_ref[...] = rows[: group * chunk].reshape(o_ref.shape).astype(jnp.bfloat16)
 
 
 def real_sums(re, im):
@@ -222,7 +222,7 @@
     padded = -(-lines // SLAB) * SLAB
     for m in range(members):
         rows[m * depth : (m + 1) * depth] = sum(d_ref[m, h].astype(jnp.float32) for h in range(hours))
-    if padded > lines:
+    if rows.shape[0] > members * depth:
         rows[members * depth :] = jnp.zeros((rows.shape[0] - members * depth, LANES), jnp.float32)
     half = pieces // 2
     daily = []
@@ -316,14 +316,14 @@
         functools.partial(cross_kernel, segments, share, near),
         pltpu.VMEM((hours * near, chunk_out, LANES), jnp.bfloat16),
         [VMEM],
-        [pltpu.VMEM((hours * near * chunk_out, LANES), jnp.float32)],
+        [pltpu.VMEM(((hours * near + 1) * chunk_out, LANES), jnp.float32)],
     )(every.reshape(late, stations, chunk_in + SLAB, LANES))
 
     order = second_order(hours, near)
     groups = [[t * stations + s + m for t, m in order] for s in range(0, stations, near)]
     whole = lax.all_to_all(daily, MESH_AXES, 0, 0, tiled=True, axis_index_groups=groups)
 
-    overrun = -(share * parts * parts) % SLAB * 2 * halves
+    overrun = (-(share * parts * parts) % SLAB + 2) * 2 * halves
     result = kernel_call(
         functools.partial(lag_kernel, shards, share),
         jax.ShapeDtypeStruct((parts, parts, share, 2 * bins), jnp.bfloat16),

time: 24.5 us -> 24.5 us (level)
  no operation moved by 1% of the time
where the time goes in v9:
time: 24.5 us; the launch traced here: 24.3 us
  blocking collectives  20.8 us (85%)
  Pallas kernels  2.72 us (11%)
  between operations  0.68 us (3%)
    all_to_all x1, blocking collectives, body(): lax.all_to_all(white, MESH_AXES, 0, 0, tiled=True, axis_index_groups=groups)  11.4 us
    all_to_all x1, blocking collectives, body(): lax.all_to_all(daily, MESH_AXES, 0, 0, tiled=True, axis_index_groups=groups)  9.37 us
    pallas_call x1, Pallas kernels, body(): kernel_call(functools.partial(lag_kernel, shards, share), jax.ShapeDtypeS...  1.19 us
    pallas_call x1, Pallas kernels, body(): kernel_call(functools.partial(cross_kernel, segments, share, near), pltpu...  0.79 us
    pallas_call x1, Pallas kernels, body(): kernel_call(functools.partial(whiten_kernel, classes, shards, segments),...  0.7 us

profile of v9, /device:TPU:0, one launch (start us, length us, event | category | flops | bytes accessed | tf_op | source)
XLA Modules:
  0.0 24.3 jit_solution(12398616853591001034)
XLA Ops:
  0.0 0.0 copy-start
  0.7 0.1 copy-done
  0.8 0.7 %shard_map.47 = bf16[16,32,128]{2,1,0:T(8,128)(2,1)S(1)} custom-call(bf16[6,2,2048]{2,1,0:T(2,128)(2,1)S(1)} %bitcast.11, s32[2,8]{1,0:T(2,128)} %bitcast.12, s32[1]{0:T(128)S(6)} %copy.5.count_ref, bf16[384,128]{1,0:T(8,128)(2,1)S(1)} %shard_map.46.band_ref), custom_call_target="tpu_custom_call" | custom-call | flops 1000000000 | bytes 4000000 | tf_op jit(solution)/shard_map/pallas_call | solution.py:297
  1.5 11.4 %all_to_all.10 = bf16[16,32,128]{2,1,0:T(8,128)(2,1)S(1)} all-to-all(bf16[16,32,128]{2,1,0:T(8,128)(2,1)S(1)} %shard_map.47), channel_id=1, replica_groups={{13,12,11,10,9,8,15,14,5,4,3,2,1,0,7,6},{29,28,27,26,25,24,31,30,21,20,..., dimensions={0} | all-to-all | bytes 262144 | tf_op jit(solution)/shard_map/all_to_all | solution.py:313
  12.9 0.8 %shard_map.48 = bf16[16,72,128]{2,1,0:T(8,128)(2,1)S(1)} custom-call(bf16[2,8,32,128]{3,2,1,0:T(8,128)(2,1)S(1)} %bitcast.10), custom_call_target="tpu_custom_call" | custom-call | flops 1000000000 | bytes 4000000 | tf_op jit(solution)/shard_map/pallas_call | solution.py:315
  13.7 0.0 copy-start.1
  13.7 9.4 %all_to_all.11 = bf16[16,72,128]{2,1,0:T(8,128)(2,1)S(1)} all-to-all(bf16[16,72,128]{2,1,0:T(8,128)(2,1)S(1)} %shard_map.48), channel_id=1, replica_groups={{27,19,11,3,25,17,9,1,26,18,10,2,24,16,8,0},{31,23,15,7,29,21,13,5,30,2..., dimensions={0} | all-to-all | bytes 589824 | tf_op jit(solution)/shard_map/all_to_all | solution.py:324
  23.1 0.0 copy-done.1
  23.1 1.2 %shard_map.49 = bf16[3,3,2,4096]{3,2,1,0:T(2,128)(2,1)} custom-call(bf16[4,2,144,128]{3,2,1,0:T(8,128)(2,1)S(1)} %bitcast.9, bf16[272,1024]{1,0:T(8,128)(2,1)S(1)} %copy-done.1), custom_call_target="tpu_custom_call" | custom-call | flops 1000000000 | bytes 4000000 | tf_op jit(solution)/shard_map/pallas_call | solution.py:327
  (1 shorter events, 0.0 us)
Async XLA Ops:
  0.0 0.8 %copy-start = (bf16[1,1,2,3,2,2048]{5,4,3,2,1,0:T(2,128)(2,1)S(1)}, bf16[1,1,2,3,2,2048]{5,4,3,2,1,0:T(2,128)(2,1)}, u32[]{:S(2)}) copy-start(bf16[1,1,2,3,2,2048]{5,4,3,2,1,0:T(2,128)(2,1)} %param.4) | copy-start | bytes 147460
  13.7 9.4 %copy-start.1 = (bf16[272,1024]{1,0:T(8,128)(2,1)S(1)}, bf16[272,1024]{1,0:T(8,128)(2,1)}, u32[]{:S(2)}) copy-start(bf16[272,1024]{1,0:T(8,128)(2,1)} %constant.2.clone.table_ref) | copy-start | bytes 1671172

commit v10 on v9

--- a/solution.py
+++ b/solution.py
@@ -224,25 +224,19 @@
         rows[m * depth : (m + 1) * depth] = sum(d_ref[m, h].astype(jnp.float32) for h in range(hours))
     if rows.shape[0] > members * depth:
         rows[members * depth :] = jnp.zeros((rows.shape[0] - members * depth, LANES), jnp.float32)
-    half = pieces // 2
     daily = []
-    for c in range(2):
-        for d in range(shards):
-            first = d * lines * pieces + c * half
-            line = [rows[pl.ds(first + j, padded, stride=pieces), :] for j in range(half)]
-            daily.append(jnp.concatenate(line, axis=1))
+    for d in range(shards):
+        first = d * lines * pieces
+        line = [rows[pl.ds(first + k, padded, stride=pieces), :] for k in range(pieces)]
+        daily.append(jnp.concatenate(line, axis=1))
     daily = jnp.concatenate(daily, axis=0).astype(jnp.bfloat16)
-    run = period // 2
-    middle = jnp.dot(daily, table_ref[:run], preferred_element_type=jnp.float32)
-    turn = table_ref[run : run + 2 * shards].astype(jnp.float32)
+    middle = jnp.dot(daily, table_ref[:period], preferred_element_type=jnp.float32)
+    turn = table_ref[period : period + 2 * shards].astype(jnp.float32)
     turn = turn[:shards] + turn[shards:]
-    total = shards * padded
     re, im = [], []
     for d in range(shards):
-        first = d * padded
-        with_re, with_im = middle[first : first + padded], middle[total + first : total + first + padded]
-        x = with_re[:, :period] - with_im[:, period:]
-        y = with_re[:, period:] + with_im[:, :period]
+        x = middle[d * padded : (d + 1) * padded, :period]
+        y = middle[d * padded : (d + 1) * padded, period:]
         cos, sin = turn[d : d + 1, :period], turn[d : d + 1, period:]
         re.append(x * cos - y * sin)
         im.append(x * sin + y * cos)
@@ -272,7 +266,8 @@
 
     fine = turns(d * b * (2.0 * math.pi / lags)) * bins**-0.5
     high = fine.astype(jnp.bfloat16).astype(np.float64)
-    table = np.concatenate([turns((k * b % period) * (2.0 * math.pi / period)), high, fine - high])
+    angle = (k * b % period) * (2.0 * math.pi / period)
+    table = np.concatenate([turns(angle), turns(angle + math.pi / 2), high, fine - high])
     return jnp.asarray(table, jnp.bfloat16)
 
 

time: 24.5 us -> 24.4 us (level)
  no operation moved by 1% of the time
where the time goes in v10:
time: 24.4 us; the launch traced here: 24.1 us
  blocking collectives  20.6 us (84%)
  Pallas kernels  2.69 us (11%)
  between operations  0.67 us (3%)
    all_to_all x1, blocking collectives, body(): lax.all_to_all(white, MESH_AXES, 0, 0, tiled=True, axis_index_groups=groups)  11.4 us
    all_to_all x1, blocking collectives, body(): lax.all_to_all(daily, MESH_AXES, 0, 0, tiled=True, axis_index_groups=groups)  9.24 us
    pallas_call x1, Pallas kernels, body(): kernel_call(functools.partial(lag_kernel, shards, share), jax.ShapeDtypeS...  1.16 us
    pallas_call x1, Pallas kernels, body(): kernel_call(functools.partial(cross_kernel, segments, share, near), pltpu...  0.79 us
    pallas_call x1, Pallas kernels, body(): kernel_call(functools.partial(whiten_kernel, classes, shards, segments),...  0.7 us

profile of v10, /device:TPU:0, one launch (start us, length us, event | category | flops | bytes accessed | tf_op | source)
XLA Modules:
  0.0 24.1 jit_solution(772295005128072674)
XLA Ops:
  0.0 0.0 copy-start
  0.7 0.1 copy-done
  0.8 0.7 %shard_map.47 = bf16[16,32,128]{2,1,0:T(8,128)(2,1)S(1)} custom-call(bf16[6,2,2048]{2,1,0:T(2,128)(2,1)S(1)} %bitcast.11, s32[2,8]{1,0:T(2,128)} %bitcast.12, s32[1]{0:T(128)S(6)} %copy.5.count_ref, bf16[384,128]{1,0:T(8,128)(2,1)S(1)} %shard_map.46.band_ref), custom_call_target="tpu_custom_call" | custom-call | flops 1000000000 | bytes 4000000 | tf_op jit(solution)/shard_map/pallas_call | solution.py:292
  1.5 11.4 %all_to_all.10 = bf16[16,32,128]{2,1,0:T(8,128)(2,1)S(1)} all-to-all(bf16[16,32,128]{2,1,0:T(8,128)(2,1)S(1)} %shard_map.47), channel_id=1, replica_groups={{13,12,11,10,9,8,15,14,5,4,3,2,1,0,7,6},{29,28,27,26,25,24,31,30,21,20,..., dimensions={0} | all-to-all | bytes 262144 | tf_op jit(solution)/shard_map/all_to_all | solution.py:308
  12.9 0.0 copy-start.1
  12.9 0.8 %shard_map.48 = bf16[16,72,128]{2,1,0:T(8,128)(2,1)S(1)} custom-call(bf16[2,8,32,128]{3,2,1,0:T(8,128)(2,1)S(1)} %bitcast.10), custom_call_target="tpu_custom_call" | custom-call | flops 1000000000 | bytes 4000000 | tf_op jit(solution)/shard_map/pallas_call | solution.py:310
  13.7 9.2 %all_to_all.11 = bf16[16,72,128]{2,1,0:T(8,128)(2,1)S(1)} all-to-all(bf16[16,72,128]{2,1,0:T(8,128)(2,1)S(1)} %shard_map.48), channel_id=1, replica_groups={{27,19,11,3,25,17,9,1,26,18,10,2,24,16,8,0},{31,23,15,7,29,21,13,5,30,2..., dimensions={0} | all-to-all | bytes 589824 | tf_op jit(solution)/shard_map/all_to_all | solution.py:319
  23.0 0.0 copy-done.1
  23.0 1.2 %shard_map.49 = bf16[3,3,2,4096]{3,2,1,0:T(2,128)(2,1)} custom-call(bf16[4,2,144,128]{3,2,1,0:T(8,128)(2,1)S(1)} %bitcast.9, bf16[528,1024]{1,0:T(8,128)(2,1)S(1)} %copy-done.1), custom_call_target="tpu_custom_call" | custom-call | flops 1000000000 | bytes 4000000 | tf_op jit(solution)/shard_map/pallas_call | solution.py:322
  (1 shorter events, 0.0 us)
Async XLA Ops:
  0.0 0.8 %copy-start = (bf16[1,1,2,3,2,2048]{5,4,3,2,1,0:T(2,128)(2,1)S(1)}, bf16[1,1,2,3,2,2048]{5,4,3,2,1,0:T(2,128)(2,1)}, u32[]{:S(2)}) copy-start(bf16[1,1,2,3,2,2048]{5,4,3,2,1,0:T(2,128)(2,1)} %param.4) | copy-start | bytes 147460
  12.9 10.0 %copy-start.1 = (bf16[528,1024]{1,0:T(8,128)(2,1)S(1)}, bf16[528,1024]{1,0:T(8,128)(2,1)}, u32[]{:S(2)}) copy-start(bf16[528,1024]{1,0:T(8,128)(2,1)} %constant.2.clone.table_ref) | copy-start | bytes 3244036

commit v11 on v10

--- a/solution.py
+++ b/solution.py
@@ -70,9 +70,8 @@
     stacked = jnp.concatenate(blocks, axis=0)
     high = stacked.astype(jnp.bfloat16)
     low = (stacked - high.astype(jnp.float32)).astype(jnp.bfloat16)
-    window = jnp.dot(high, band, preferred_element_type=jnp.float32) + jnp.dot(
-        low, band, preferred_element_type=jnp.float32
-    )
+    window = jnp.dot(jnp.concatenate([high, low], axis=0), band, preferred_element_type=jnp.float32)
+    window = window[: stacked.shape[0]] + window[stacked.shape[0] :]
     halves = tiles // shards
     for g in range(segments):
         for j in range(halves):
@@ -94,14 +93,15 @@
                     mixed = pltpu.roll(mixed, LANES - d, 1)
                 rows[d, first : first + 2 * PARTS] = mixed[: 2 * PARTS]
     packed = rows[...].astype(jnp.bfloat16)
+    lines = rows.shape[1]
+    for place, d in enumerate(classes):
+        o_ref[place, :lines] = packed[d]
     pairs_copy.wait()
     slots = pairs.shape[1]
     lists = jnp.concatenate([pairs[...].astype(jnp.float32), jnp.zeros((2, LANES - slots), jnp.float32)], axis=1)
     counts = jnp.full((SLAB - 2, LANES), count_ref[0].astype(jnp.float32))
     lists = jnp.concatenate([lists, counts], axis=0).astype(jnp.bfloat16)
-    lines = rows.shape[1]
-    for place, d in enumerate(classes):
-        o_ref[place, :lines] = packed[d]
+    for place in range(len(classes)):
         o_ref[place, lines:] = lists
 
 

time: 24.4 us -> 24.4 us (level)
  no operation moved by 1% of the time
where the time goes in v11:
time: 24.4 us; the launch traced here: 24.1 us
  blocking collectives  20.6 us (84%)
  Pallas kernels  2.7 us (11%)
  between operations  0.67 us (3%)
    all_to_all x1, blocking collectives, body(): lax.all_to_all(white, MESH_AXES, 0, 0, tiled=True, axis_index_groups=groups)  11.4 us
    all_to_all x1, blocking collectives, body(): lax.all_to_all(daily, MESH_AXES, 0, 0, tiled=True, axis_index_groups=groups)  9.23 us
    pallas_call x1, Pallas kernels, body(): kernel_call(functools.partial(lag_kernel, shards, share), jax.ShapeDtypeS...  1.17 us
    pallas_call x1, Pallas kernels, body(): kernel_call(functools.partial(cross_kernel, segments, share, near), pltpu...  0.79 us
    pallas_call x1, Pallas kernels, body(): kernel_call(functools.partial(whiten_kernel, classes, shards, segments),...  0.7 us

profile of v11, /device:TPU:0, one launch (start us, length us, event | category | flops | bytes accessed | tf_op | source)
XLA Modules:
  0.0 24.1 jit_solution(4954733763380834897)
XLA Ops:
  0.0 0.0 copy-start
  0.7 0.1 copy-done
  0.8 0.7 %shard_map.47 = bf16[16,32,128]{2,1,0:T(8,128)(2,1)S(1)} custom-call(bf16[6,2,2048]{2,1,0:T(2,128)(2,1)S(1)} %bitcast.11, s32[2,8]{1,0:T(2,128)} %bitcast.12, s32[1]{0:T(128)S(6)} %copy.5.count_ref, bf16[384,128]{1,0:T(8,128)(2,1)S(1)} %shard_map.46.band_ref), custom_call_target="tpu_custom_call" | custom-call | flops 1000000000 | bytes 4000000 | tf_op jit(solution)/shard_map/pallas_call | solution.py:292
  1.5 11.4 %all_to_all.10 = bf16[16,32,128]{2,1,0:T(8,128)(2,1)S(1)} all-to-all(bf16[16,32,128]{2,1,0:T(8,128)(2,1)S(1)} %shard_map.47), channel_id=1, replica_groups={{13,12,11,10,9,8,15,14,5,4,3,2,1,0,7,6},{29,28,27,26,25,24,31,30,21,20,..., dimensions={0} | all-to-all | bytes 262144 | tf_op jit(solution)/shard_map/all_to_all | solution.py:308
  12.9 0.0 copy-start.1
  12.9 0.8 %shard_map.48 = bf16[16,72,128]{2,1,0:T(8,128)(2,1)S(1)} custom-call(bf16[2,8,32,128]{3,2,1,0:T(8,128)(2,1)S(1)} %bitcast.10), custom_call_target="tpu_custom_call" | custom-call | flops 1000000000 | bytes 4000000 | tf_op jit(solution)/shard_map/pallas_call | solution.py:310
  13.7 9.2 %all_to_all.11 = bf16[16,72,128]{2,1,0:T(8,128)(2,1)S(1)} all-to-all(bf16[16,72,128]{2,1,0:T(8,128)(2,1)S(1)} %shard_map.48), channel_id=1, replica_groups={{27,19,11,3,25,17,9,1,26,18,10,2,24,16,8,0},{31,23,15,7,29,21,13,5,30,2..., dimensions={0} | all-to-all | bytes 589824 | tf_op jit(solution)/shard_map/all_to_all | solution.py:319
  22.9 0.0 copy-done.1
  23.0 1.2 %shard_map.49 = bf16[3,3,2,4096]{3,2,1,0:T(2,128)(2,1)} custom-call(bf16[4,2,144,128]{3,2,1,0:T(8,128)(2,1)S(1)} %bitcast.9, bf16[528,1024]{1,0:T(8,128)(2,1)S(1)} %copy-done.1), custom_call_target="tpu_custom_call" | custom-call | flops 1000000000 | bytes 4000000 | tf_op jit(solution)/shard_map/pallas_call | solution.py:322
  (1 shorter events, 0.0 us)
Async XLA Ops:
  0.0 0.8 %copy-start = (bf16[1,1,2,3,2,2048]{5,4,3,2,1,0:T(2,128)(2,1)S(1)}, bf16[1,1,2,3,2,2048]{5,4,3,2,1,0:T(2,128)(2,1)}, u32[]{:S(2)}) copy-start(bf16[1,1,2,3,2,2048]{5,4,3,2,1,0:T(2,128)(2,1)} %param.4) | copy-start | bytes 147460
  12.9 10.0 %copy-start.1 = (bf16[528,1024]{1,0:T(8,128)(2,1)S(1)}, bf16[528,1024]{1,0:T(8,128)(2,1)}, u32[]{:S(2)}) copy-start(bf16[528,1024]{1,0:T(8,128)(2,1)} %constant.2.clone.table_ref) | copy-start | bytes 3244036

commit v12 on v11

--- a/solution.py
+++ b/solution.py
@@ -242,11 +242,9 @@
         im.append(x * sin + y * cos)
     sums = real_sums(re, im)
     for a in range(shards):
-        value = sums[(a + shards // 2) % shards]
+        value = sums[(a + shards // 2) % shards].astype(jnp.bfloat16)
         for n in range(PARTS * PARTS):
-            lags_ref[n // PARTS, n % PARTS, :, a * period : (a + 1) * period] = value[n * share : (n + 1) * share].astype(
-                jnp.bfloat16
-            )
+            lags_ref[n // PARTS, n % PARTS, :, a * period : (a + 1) * period] = value[n * share : (n + 1) * share]
     copy = pltpu.make_async_copy(lags_ref, o_ref, sem)
     copy.start()
     copy.wait()

time: 24.4 us -> 24.4 us (level)
  no operation moved by 1% of the time
where the time goes in v12:
time: 24.4 us; the launch traced here: 24.1 us
  blocking collectives  20.6 us (84%)
  Pallas kernels  2.7 us (11%)
  between operations  0.67 us (3%)
    all_to_all x1, blocking collectives, body(): lax.all_to_all(white, MESH_AXES, 0, 0, tiled=True, axis_index_groups=groups)  11.4 us
    all_to_all x1, blocking collectives, body(): lax.all_to_all(daily, MESH_AXES, 0, 0, tiled=True, axis_index_groups=groups)  9.23 us
    pallas_call x1, Pallas kernels, body(): kernel_call(functools.partial(lag_kernel, shards, share), jax.ShapeDtypeS...  1.17 us
    pallas_call x1, Pallas kernels, body(): kernel_call(functools.partial(cross_kernel, segments, share, near), pltpu...  0.79 us
    pallas_call x1, Pallas kernels, body(): kernel_call(functools.partial(whiten_kernel, classes, shards, segments),...  0.7 us

profile of v12, /device:TPU:0, one launch (start us, length us, event | category | flops | bytes accessed | tf_op | source)
XLA Modules:
  0.0 24.1 jit_solution(4954733763380834897)
XLA Ops:
  0.0 0.0 copy-start
  0.7 0.1 copy-done
  0.8 0.7 %shard_map.47 = bf16[16,32,128]{2,1,0:T(8,128)(2,1)S(1)} custom-call(bf16[6,2,2048]{2,1,0:T(2,128)(2,1)S(1)} %bitcast.11, s32[2,8]{1,0:T(2,128)} %bitcast.12, s32[1]{0:T(128)S(6)} %copy.5.count_ref, bf16[384,128]{1,0:T(8,128)(2,1)S(1)} %shard_map.46.band_ref), custom_call_target="tpu_custom_call" | custom-call | flops 1000000000 | bytes 4000000 | tf_op jit(solution)/shard_map/pallas_call | solution.py:290
  1.5 11.4 %all_to_all.10 = bf16[16,32,128]{2,1,0:T(8,128)(2,1)S(1)} all-to-all(bf16[16,32,128]{2,1,0:T(8,128)(2,1)S(1)} %shard_map.47), channel_id=1, replica_groups={{13,12,11,10,9,8,15,14,5,4,3,2,1,0,7,6},{29,28,27,26,25,24,31,30,21,20,..., dimensions={0} | all-to-all | bytes 262144 | tf_op jit(solution)/shard_map/all_to_all | solution.py:306
  12.9 0.0 copy-start.1
  12.9 0.8 %shard_map.48 = bf16[16,72,128]{2,1,0:T(8,128)(2,1)S(1)} custom-call(bf16[2,8,32,128]{3,2,1,0:T(8,128)(2,1)S(1)} %bitcast.10), custom_call_target="tpu_custom_call" | custom-call | flops 1000000000 | bytes 4000000 | tf_op jit(solution)/shard_map/pallas_call | solution.py:308
  13.7 9.2 %all_to_all.11 = bf16[16,72,128]{2,1,0:T(8,128)(2,1)S(1)} all-to-all(bf16[16,72,128]{2,1,0:T(8,128)(2,1)S(1)} %shard_map.48), channel_id=1, replica_groups={{27,19,11,3,25,17,9,1,26,18,10,2,24,16,8,0},{31,23,15,7,29,21,13,5,30,2..., dimensions={0} | all-to-all | bytes 589824 | tf_op jit(solution)/shard_map/all_to_all | solution.py:317
  22.9 0.0 copy-done.1
  23.0 1.2 %shard_map.49 = bf16[3,3,2,4096]{3,2,1,0:T(2,128)(2,1)} custom-call(bf16[4,2,144,128]{3,2,1,0:T(8,128)(2,1)S(1)} %bitcast.9, bf16[528,1024]{1,0:T(8,128)(2,1)S(1)} %copy-done.1), custom_call_target="tpu_custom_call" | custom-call | flops 1000000000 | bytes 4000000 | tf_op jit(solution)/shard_map/pallas_call | solution.py:320
  (1 shorter events, 0.0 us)
Async XLA Ops:
  0.0 0.8 %copy-start = (bf16[1,1,2,3,2,2048]{5,4,3,2,1,0:T(2,128)(2,1)S(1)}, bf16[1,1,2,3,2,2048]{5,4,3,2,1,0:T(2,128)(2,1)}, u32[]{:S(2)}) copy-start(bf16[1,1,2,3,2,2048]{5,4,3,2,1,0:T(2,128)(2,1)} %param.4) | copy-start | bytes 147460
  12.9 10.0 %copy-start.1 = (bf16[528,1024]{1,0:T(8,128)(2,1)S(1)}, bf16[528,1024]{1,0:T(8,128)(2,1)}, u32[]{:S(2)}) copy-start(bf16[528,1024]{1,0:T(8,128)(2,1)} %constant.2.clone.table_ref) | copy-start | bytes 3244036
